TPU v7x, 1024 devices: a whole 4x8x16 slice. The times are simulated.
1024 devices in a mesh: rows: 128 (over x, z, core), cols: 8 (over y).
Axes of the slice: x: 4, y: 8, z: 16, core: 2. Of those that a mesh axis runs over, the one named last changes fastest.
Arguments:
- field: float32 [1024, 256, 128], P('rows', 'cols'), may hold values from -6 to 6
- filter_first: float32 [3, 3, 128, 128], replicated, may hold values from -0.1875 to 0.1875
- filter_second: float32 [3, 3, 128, 128], replicated, may hold values from -0.1875 to 0.1875
- cotangent: float32 [1024, 256, 128], P('rows', 'cols'), may hold values from -6 to 6
Outputs:
- input_grad: float32 [1024, 256, 128], P('rows', 'cols')
- first_grad: float32 [3, 3, 128, 128], replicated
- second_grad: float32 [3, 3, 128, 128], replicated
All inputs are finite; a program needn't handle non-finite values.
Results may differ from a plain program's by a relative error of at most 0.0003.
Values sent between devices are 32-bit elements; how exact they have to be, the bound alone decides.
No kernel may reach another device: no remote copies, remote signals or barrier semaphores. Data moves between devices by JAX's collectives and lax.ppermute only.
A program may use at most 32 MiB of HBM per device.

v0:
```python
import math

import jax
import jax.numpy as jnp
from jax import lax
from jax.sharding import PartitionSpec as P


def extended(block, sides, width):
    for axis, dim in sides:
        count = lax.axis_size(axis)
        forward = [(i, i + 1) for i in range(count - 1)]
        backward = [(target, source) for source, target in forward]
        low = lax.ppermute(
            lax.slice_in_dim(block, block.shape[dim] - width, None, axis=dim), axis, forward
        )
        high = lax.ppermute(lax.slice_in_dim(block, 0, width, axis=dim), axis, backward)
        block = jnp.concatenate([low, block, high], axis=dim)
    return block


def thin_halo(values):
    return extended(values, (("rows", 0), ("cols", 1)), 1)


def shifted_product(padded, kernel):
    out_rows = padded.shape[0] - 2
    out_cols = padded.shape[1] - 2
    summed = None
    for row_shift in range(3):
        stripe = padded[row_shift : row_shift + out_rows]
        stacked = jnp.concatenate(
            [stripe[:, col_shift : col_shift + out_cols] for col_shift in range(3)], axis=2
        )
        partial_sum = jnp.dot(
            stacked.reshape(out_rows * out_cols, -1),
            kernel[row_shift].reshape(-1, kernel.shape[3]),
            precision=lax.Precision.HIGHEST,
            preferred_element_type=jnp.float32,
        )
        summed = partial_sum if summed is None else summed + partial_sum
    return summed.reshape(out_rows, out_cols, -1)


def flipped(kernel):
    return jnp.transpose(jnp.flip(kernel, (0, 1)), (0, 1, 3, 2))


def filter_product(padded, deltas):
    out_rows, out_cols, channels = deltas.shape
    flat_delta = deltas.reshape(out_rows * out_cols, channels)
    outer = []
    for row_shift in range(3):
        inner = []
        for col_shift in range(3):
            window = padded[
                row_shift : row_shift + out_rows, col_shift : col_shift + out_cols
            ].reshape(out_rows * out_cols, -1)
            inner.append(
                lax.dot_general(
                    window,
                    flat_delta,
                    (((0,), (0,)), ((), ())),
                    precision=lax.Precision.HIGHEST,
                    preferred_element_type=jnp.float32,
                )
            )
        outer.append(jnp.stack(inner))
    return jnp.stack(outer)


def silu_slope(values):
    sigmoid = jax.nn.sigmoid(values)
    return sigmoid * (1.0 + values * (1.0 - sigmoid))


def local(field, filter_first, filter_second, cotangent):
    tile_rows, tile_cols, channels = field.shape
    pixels = tile_rows * tile_cols * lax.axis_size("rows") * lax.axis_size("cols")
    factor = 1.0 / math.sqrt(pixels)
    near_field = thin_halo(field)
    first_pre = shifted_product(near_field, filter_first)
    hidden_pad = thin_halo(jax.nn.silu(first_pre))
    second_pre = shifted_product(hidden_pad, filter_second)
    second_delta = cotangent * silu_slope(second_pre)
    second_grad = filter_product(hidden_pad, second_delta) * factor
    back_pre = shifted_product(thin_halo(second_delta), flipped(filter_second))
    first_delta = back_pre * silu_slope(first_pre)
    first_delta_pad = thin_halo(first_delta)
    first_grad = filter_product(near_field, first_delta) * factor
    input_grad = shifted_product(first_delta_pad, flipped(filter_first))
    first_grad, second_grad = lax.psum((first_grad, second_grad), ("rows", "cols"))
    return (input_grad, first_grad, second_grad)


def solution(mesh):
    in_specs = (P("rows", "cols", None), P(), P(), P("rows", "cols", None))
    out_specs = (P("rows", "cols", None), P(), P())
    return jax.shard_map(local, mesh=mesh, in_specs=in_specs, out_specs=out_specs, check_vma=False)
```

profile of v0, /device:TPU:1, one launch (start us, length us, event | category | flops | bytes accessed | tf_op | source)
XLA Modules:
  0.0 597.6 jit_solution(16910752327653206822)
XLA Ops:
  7.9 5.4 collective-permute-start
  13.3 12.1 %collective-permute-start.1 = (f32[1,32,128]{2,1,0:T(8,128)S(1)}, f32[1,32,128]{2,1,0:T(8,128)S(1)}, u32[]{:S(2)}, u32[]{:S(2)}) collective-permute-start(f32[1,32,128]{2,1,0:T(8,128)S(1)} %get-tuple-element.76), channel_id=1, source_target_pairs={{8,0},{16,8},{24,16},{32,24},{40,32},{48,40},{56,48},{64,56},{72,6... | collective-permute-start | bytes 49160 | tf_op jit(solution)/shard_map/ppermute | solution.py:17
  30.7 1.3 collective-permute-start.3
  32.4 2.8 collective-permute-done.3
  37.4 1.9 collective-permute-start.4
  39.3 2.4 collective-permute-start.5
  41.8 2.6 collective-permute-done.5
  44.4 2.0 collective-permute-start.6
  46.4 1.3 collective-permute-start.7
  47.8 3.0 collective-permute-done.7
  55.7 3.4 collective-permute-start.8
  59.0 1.9 collective-permute-start.9
  61.8 2.3 collective-permute-done.9
  64.1 1.6 collective-permute-start.10
  65.8 1.5 collective-permute-start.11
  68.1 2.0 collective-permute-done.11
  75.9 3.4 collective-permute-start.12
  79.3 1.9 collective-permute-start.13
  81.3 3.0 collective-permute-done.13
  84.3 3.3 collective-permute-start.14
  87.6 1.3 collective-permute-start.15
  89.8 2.2 collective-permute-done.15
  94.3 493.7 %all-reduce.3.cloned.1.call-done = (f32[3,3,128,128]{3,2,1,0:T(8,128)}, f32[3,3,128,128]{3,2,1,0:T(8,128)}) async-done(((f32[3,3,128,128]{3,2,1,0:T(8,128)}, f32[3,3,128,128]{3,2,1,0:T(8,128)}), (f32[3,3,128,128]{3,2,1,0:T(8,128)}, f32[3,3,128,128]{3,2,1,0:T(8,128)})) %all-reduce.3.cloned.1.call-update) | async-done | bytes 1179664 | tf_op jit(solution)/shard_map/psum | solution.py:92
  587.9 2.0 copy.19
  (110 shorter events, 24.7 us)
Async XLA Ops:
  7.2 580.8 %all-reduce.3.cloned.1.call-start = ((), (), s32[]{:S(2)}) async-start(), calls=%async_computation | async-start | bytes 2359296 | tf_op jit(solution)/shard_map/psum | solution.py:92
  7.9 20.5 %collective-permute-start = (f32[1,32,128]{2,1,0:T(8,128)S(1)}, f32[1,32,128]{2,1,0:T(8,128)S(1)}, u32[]{:S(2)}, u32[]{:S(2)}) collective-permute-start(f32[1,32,128]{2,1,0:T(8,128)S(1)} %get-tuple-element.77), channel_id=1, source_target_pairs={{0,8},{8,16},{16,24},{24,32},{32,40},{40,48},{48,56},{56,64},{64,7... | collective-permute-start | bytes 49160 | tf_op jit(solution)/shard_map/ppermute | solution.py:14
  13.3 13.3 %copy-start = (f32[3,3,128,128]{3,2,1,0:T(8,128)S(1)}, f32[3,3,128,128]{3,2,1,0:T(8,128)}, u32[]{:S(2)}) copy-start(f32[3,3,128,128]{3,2,1,0:T(8,128)} %param.6) | copy-start | bytes 1769476
  13.3 16.0 %collective-permute-start.1 = (f32[1,32,128]{2,1,0:T(8,128)S(1)}, f32[1,32,128]{2,1,0:T(8,128)S(1)}, u32[]{:S(2)}, u32[]{:S(2)}) collective-permute-start(f32[1,32,128]{2,1,0:T(8,128)S(1)} %get-tuple-element.76), channel_id=1, source_target_pairs={{8,0},{16,8},{24,16},{32,24},{40,32},{48,40},{56,48},{64,56},{72,6... | collective-permute-start | bytes 49160 | tf_op jit(solution)/shard_map/ppermute | solution.py:17
  26.6 1.1 copy-start.1
  29.4 3.0 copy-start.5
  29.4 2.7 copy-start.7
  29.4 2.9 collective-permute-start.2
  30.7 4.5 collective-permute-start.3
  32.3 2.9 copy-start.8
  35.4 0.9 copy-start.3
  37.4 4.4 collective-permute-start.4
  39.3 5.1 collective-permute-start.5
  44.4 3.4 collective-permute-start.6
  46.4 4.4 collective-permute-start.7
  55.7 6.2 %collective-permute-start.8 = (f32[1,32,128]{2,1,0:T(8,128)S(1)}, f32[1,32,128]{2,1,0:T(8,128)S(1)}, u32[]{:S(2)}, u32[]{:S(2)}) collective-permute-start(f32[1,32,128]{2,1,0:T(8,128)S(1)} %get-tuple-element.67), channel_id=1, source_target_pairs={{0,8},{8,16},{16,24},{24,32},{32,40},{40,48},{48,56},{56,64},{64,7... | collective-permute-start | bytes 49160 | tf_op jit(solution)/shard_map/ppermute | solution.py:14
  59.0 5.1 collective-permute-start.9
  64.1 4.0 collective-permute-start.10
  65.8 4.4 collective-permute-start.11
  75.9 5.4 collective-permute-start.12
  79.3 5.1 collective-permute-start.13
  84.3 5.5 collective-permute-start.14
  87.6 4.4 collective-permute-start.15
  587.9 2.0 copy-start.4
  (3 other events, 2.7 us)
Sparse Core Ops, SparseCore 0:
  89.9 497.9 all-reduce.2
where the time goes:
time: 598 us
  waiting for transfers between devices  512 us (86%)
  starting transfers between devices  46 us (8%)
  between operations  14.7 us (2%)
  matrix products  13.3 us (2%)
  local copies, waits for them, and re-layouts  9.41 us (2%)
    psum x1, waiting for transfers between devices, local(): lax.psum((first_grad, second_grad), ('rows', 'cols'))  494 us
    ppermute x8, starting transfers between devices, extended(): lax.ppermute(lax.slice_in_dim(block, 0, width, axis=dim), axis, backward)  23.7 us
    ppermute x8, starting transfers between devices, extended(): lax.ppermute(lax.slice_in_dim(block, block.shape[dim] - width, None, axis...  22.2 us
    ppermute x8, waiting for transfers between devices, extended(): lax.ppermute(lax.slice_in_dim(block, 0, width, axis=dim), axis, backward)  17.9 us
  transfers between devices with their start and end apart: 17, of which 8 were waited for; matrix products, arithmetic and copies ran while one was open for 1% of the time, Pallas kernels for 0%

commit v1 on v0

v1 whole, which is shorter than its diff:
```python
import math

import jax
import jax.numpy as jnp
from jax import lax
from jax.sharding import Mesh, PartitionSpec as P

ROWS = ("x", "z", "core")
FIELD_HALO = 4
COT_HALO = 2


def neighbours(values, axis):
    count = lax.axis_size(axis)
    forward = [(i, i + 1) for i in range(count - 1)]
    backward = [(target, source) for source, target in forward]
    low, high = values
    return lax.ppermute(low, axis, forward), lax.ppermute(high, axis, backward)


def wide_halo(field, cotangent):
    tile_rows, tile_cols, channels = field.shape
    a, b = FIELD_HALO, COT_HALO
    low, high = neighbours(
        (
            jnp.concatenate([field[-a:], cotangent[-b:]], axis=0),
            jnp.concatenate([field[:a], cotangent[:b]], axis=0),
        ),
        ROWS,
    )
    field = jnp.concatenate([low[:a], field, high[:a]], axis=0)
    cotangent = jnp.concatenate([low[a:], cotangent, high[a:]], axis=0)
    rows_f, rows_c = field.shape[0], cotangent.shape[0]

    def pack(f, c):
        return jnp.concatenate([f.reshape(-1, channels), c.reshape(-1, channels)], axis=0)

    low, high = neighbours(
        (pack(field[:, -a:], cotangent[:, -b:]), pack(field[:, :a], cotangent[:, :b])), "y"
    )

    def unpack(p):
        return p[: rows_f * a].reshape(rows_f, a, channels), p[rows_f * a :].reshape(rows_c, b, channels)

    low_f, low_c = unpack(low)
    high_f, high_c = unpack(high)
    field = jnp.concatenate([low_f, field, high_f], axis=1)
    cotangent = jnp.concatenate([low_c, cotangent, high_c], axis=1)
    return field, cotangent


def shifted_product(padded, kernel):
    out_rows = padded.shape[0] - 2
    out_cols = padded.shape[1] - 2
    summed = None
    for row_shift in range(3):
        stripe = padded[row_shift : row_shift + out_rows]
        stacked = jnp.concatenate(
            [stripe[:, col_shift : col_shift + out_cols] for col_shift in range(3)], axis=2
        )
        partial_sum = jnp.dot(
            stacked.reshape(out_rows * out_cols, -1),
            kernel[row_shift].reshape(-1, kernel.shape[3]),
            precision=lax.Precision.HIGH,
            preferred_element_type=jnp.float32,
        )
        summed = partial_sum if summed is None else summed + partial_sum
    return summed.reshape(out_rows, out_cols, -1)


def flipped(kernel):
    return jnp.transpose(jnp.flip(kernel, (0, 1)), (0, 1, 3, 2))


def filter_product(padded, deltas):
    out_rows, out_cols, channels = deltas.shape
    flat_delta = deltas.reshape(out_rows * out_cols, channels)
    outer = []
    for row_shift in range(3):
        for col_shift in range(3):
            window = padded[
                row_shift : row_shift + out_rows, col_shift : col_shift + out_cols
            ].reshape(out_rows * out_cols, -1)
            outer.append(
                lax.dot_general(
                    window,
                    flat_delta,
                    (((0,), (0,)), ((), ())),
                    precision=lax.Precision.HIGH,
                    preferred_element_type=jnp.float32,
                )
            )
    return jnp.concatenate(outer, axis=0)


def silu_slope(values):
    sigmoid = jax.nn.sigmoid(values)
    return sigmoid * (1.0 + values * (1.0 - sigmoid))


def inside(tile_rows, tile_cols, margin):
    height = tile_rows * lax.axis_size(ROWS)
    width = tile_cols * lax.axis_size("y")
    shape = (tile_rows + 2 * margin, tile_cols + 2 * margin, 1)
    row = lax.broadcasted_iota(jnp.int32, shape, 0) + lax.axis_index(ROWS) * tile_rows - margin
    col = lax.broadcasted_iota(jnp.int32, shape, 1) + lax.axis_index("y") * tile_cols - margin
    return (row >= 0) & (row < height) & (col >= 0) & (col < width)


def total(first, second):
    core = lax.axis_index("core")
    other = [(0, 1), (1, 0)]
    mine = jnp.where(core == 0, second, first)
    theirs = jnp.where(core == 0, first, second)
    with jax.named_scope("cores"):
        mine = mine + lax.ppermute(theirs, "core", other)
    channels = mine.shape[-1]
    with jax.named_scope("x_scatter"):
        n = lax.axis_size("x")
        mine = lax.all_to_all(mine.reshape(n, -1, channels), "x", 0, 0).sum(0)
    with jax.named_scope("y_scatter"):
        n = lax.axis_size("y")
        mine = lax.all_to_all(mine.reshape(n, -1, channels), "y", 0, 0).sum(0)
    with jax.named_scope("z_total"):
        mine = lax.all_gather(mine, "z", axis=0).sum(0)
    with jax.named_scope("y_gather"):
        mine = lax.all_gather(mine, "y", axis=0).reshape(-1, channels)
    with jax.named_scope("x_gather"):
        mine = lax.all_gather(mine, "x", axis=0).reshape(-1, channels)
    with jax.named_scope("cores_back"):
        theirs = lax.ppermute(mine, "core", other)
    first = jnp.where(core == 0, theirs, mine)
    second = jnp.where(core == 0, mine, theirs)
    return first, second


def local(field, filter_first, filter_second, cotangent):
    tile_rows, tile_cols, channels = field.shape
    pixels = tile_rows * tile_cols * lax.axis_size(ROWS) * lax.axis_size("y")
    factor = 1.0 / math.sqrt(pixels)
    far_field, far_cot = wide_halo(field, cotangent)
    first_pre = shifted_product(far_field, filter_first)
    hidden = jnp.where(inside(tile_rows, tile_cols, 3), jax.nn.silu(first_pre), 0.0)
    second_pre = shifted_product(hidden, filter_second)
    second_delta = far_cot * silu_slope(second_pre)
    back_pre = shifted_product(second_delta, flipped(filter_second))
    first_delta = back_pre * silu_slope(first_pre[2:-2, 2:-2])
    first_delta = jnp.where(inside(tile_rows, tile_cols, 1), first_delta, 0.0)
    second_grad = filter_product(hidden[2:-2, 2:-2], second_delta[2:-2, 2:-2]) * factor
    first_grad = filter_product(far_field[3:-3, 3:-3], first_delta[1:-1, 1:-1]) * factor
    first_grad, second_grad = total(first_grad, second_grad)
    input_grad = shifted_product(first_delta, flipped(filter_first))
    shape = filter_first.shape
    return (input_grad, first_grad.reshape(shape), second_grad.reshape(shape))


def solution(mesh):
    fine = Mesh(mesh.devices.reshape(4, 16, 2, 8), ("x", "z", "core", "y"))
    tile = P(ROWS, "y", None)
    return jax.shard_map(
        local, mesh=fine, in_specs=(tile, P(), P(), tile), out_specs=(tile, P(), P()), check_vma=False
    )
```

time: 598 us -> 177 us (0.30)
  waiting for transfers between devices: 512 us -> 20.4 us
  blocking collectives: 0 us -> 50.7 us
  starting transfers between devices: 46 us -> 64.2 us
  between operations: 14.7 us -> 1.33 us
  local copies, waits for them, and re-layouts: 9.41 us -> 18 us
  other arithmetic: 2.57 us -> 9.04 us
    psum x1 -> x0, waiting for transfers between devices: 494 us -> none  [local(): lax.psum((first_grad, second_grad), ('rows', 'cols'))]
    all_gather x0 -> x3, blocking collectives: none -> 50.7 us  [the longest x1 21.9 us: total(): mine = lax.all_gather(mine, 'z', axis=0).sum(0)]
    all_to_all x0 -> x2, waiting for transfers between devices: none -> 17.4 us  [the longest x1 9.43 us: total(): mine = lax.all_to_all(mine.reshape(n, -1, channels), 'x', 0, 0).sum(0)]
    all_to_all x0 -> x2, starting transfers between devices: none -> 17 us  [the longest x1 8.79 us: total(): mine = lax.all_to_all(mine.reshape(n, -1, channels), 'y', 0, 0).sum(0)]
    ppermute x16 -> x6, waiting for transfers between devices: 17.9 us -> 2.97 us  [the longest x1 1.66 us: total(): mine = mine + lax.ppermute(theirs, 'core', other)]
    ppermute x16 -> x6, starting transfers between devices: 45.9 us -> 47.2 us  [the longest x1 20.4 us: total(): theirs = lax.ppermute(mine, 'core', other)]
  transfers between devices with their start and end apart: 17 -> 8, of which waited for: 8 -> 5; matrix products, arithmetic and copies ran while one was open for 1% -> 3% of each run, Pallas kernels for 0% -> 0%
where the time goes in v1:
time: 177 us; the launch traced here: 176 us
  starting transfers between devices  64.2 us (36%)
  blocking collectives  50.7 us (29%)
  waiting for transfers between devices  20.4 us (12%)
  local copies, waits for them, and re-layouts  18 us (10%)
  matrix products  12 us (7%)
  other arithmetic  9.04 us (5%)
    all_gather x1, blocking collectives, total(): mine = lax.all_gather(mine, 'z', axis=0).sum(0)  21.9 us
    ppermute x1, starting transfers between devices, total(): theirs = lax.ppermute(mine, 'core', other)  20.4 us
    all_gather x1, blocking collectives, total(): mine = lax.all_gather(mine, 'y', axis=0).reshape(-1, channels)  18.6 us
    ppermute x2, starting transfers between devices, neighbours(): lax.ppermute(high, axis, backward)  17.4 us
    all_gather x1, blocking collectives, total(): mine = lax.all_gather(mine, 'x', axis=0).reshape(-1, channels)  10.3 us
    all_to_all x1, waiting for transfers between devices, total(): mine = lax.all_to_all(mine.reshape(n, -1, channels), 'x', 0, 0).sum(0)  9.43 us
    all_to_all x1, starting transfers between devices, total(): mine = lax.all_to_all(mine.reshape(n, -1, channels), 'y', 0, 0).sum(0)  8.79 us
    unnamed x53, local copies, waits for them, and re-layouts  8.54 us
  transfers between devices with their start and end apart: 8, of which 5 were waited for; matrix products, arithmetic and copies ran while one was open for 3% of the time, Pallas kernels for 0%

profile of v1, /device:TPU:1, one launch (start us, length us, event | category | flops | bytes accessed | tf_op | source)
XLA Modules:
  0.0 175.7 jit_solution(16549032250223002245)
XLA Ops:
  1.6 16.1 %collective-permute-start.1 = (f32[6,32,128]{2,1,0:T(8,128)S(1)}, f32[6,32,128]{2,1,0:T(8,128)S(1)}, u32[]{:S(2)}, u32[]{:S(2)}) collective-permute-start(f32[6,32,128]{2,1,0:T(8,128)S(1)} %pad_maximum_fusion.15), channel_id=1, source_target_pairs={{8,0},{16,8},{24,16},{32,24},{40,32},{48,40},{56,48},{64,56},{72,6... | collective-permute-start | bytes 294920 | tf_op jit(solution)/shard_map/ppermute | solution.py:18
  17.7 1.9 %collective-permute-start = (f32[6,32,128]{2,1,0:T(8,128)S(1)}, f32[6,32,128]{2,1,0:T(8,128)S(1)}, u32[]{:S(2)}, u32[]{:S(2)}) collective-permute-start(f32[6,32,128]{2,1,0:T(8,128)S(1)} %pad_maximum_fusion.14), channel_id=1, source_target_pairs={{0,8},{8,16},{16,24},{24,32},{32,40},{40,48},{48,56},{56,64},{64,7... | collective-permute-start | bytes 294920 | tf_op jit(solution)/shard_map/ppermute | solution.py:18
  24.8 1.3 collective-permute-start.3
  26.1 4.0 %collective-permute-start.2 = (f32[88,128]{1,0:T(8,128)S(1)}, f32[88,128]{1,0:T(8,128)S(1)}, u32[]{:S(2)}, u32[]{:S(2)}) collective-permute-start(f32[88,128]{1,0:T(8,128)S(1)} %pad_maximum_fusion.16), channel_id=1, source_target_pairs={{0,1},{1,2},{2,3},{3,4},{4,5},{5,6},{6,7},{8,9},{9,10},{10,11},{11... | collective-permute-start | bytes 135176 | tf_op jit(solution)/shard_map/ppermute | solution.py:18
  30.2 1.0 collective-permute-done.2
  33.9 1.0 pad_maximum_fusion.2
  35.0 1.0 reshape.216
  38.9 0.9 reshape.218
  40.9 1.5 fusion.74
  46.0 1.0 pad_maximum_fusion.7
  47.1 1.1 pad_maximum_fusion.8
  58.7 3.5 %collective-permute-start.4 = (f32[1152,128]{1,0:T(8,128)}, f32[1152,128]{1,0:T(8,128)}, u32[]{:S(2)}, u32[]{:S(2)}) collective-permute-start(f32[1152,128]{1,0:T(8,128)} %multiply_select_fusion), channel_id=1, source_target_pairs={{0,8},{8,0},{1,9},{9,1},{2,10},{10,2},{3,11},{11,3},{4,12},{12,4},... | collective-permute-start | bytes 1769480 | tf_op jit(solution)/shard_map/cores/ppermute | solution.py:116
  62.6 1.7 collective-permute-done.4
  64.2 2.0 %select_add_fusion = f32[1152,128]{1,0:T(8,128)} fusion(f32[1152,128]{1,0:T(8,128)} %collective-permute-done.4, f32[1152,128]{1,0:T(8,128)S(1)} %fusion.2, f32[1152,128]{1,0:T(8,128)S(1)} %fusion.9, pred[]{:T(512)S(6)} %eq.2), kind=kLoop, calls=%fused_computation.53 | loop fusion | flops 589824 | bytes 2359297 | tf_op jit(solution)/shard_map/cores/add | solution.py:116
  66.2 8.2 %all-to-all-start = ((f32[4,288,128]{2,1,0:T(8,128)}), f32[4,288,128]{2,1,0:T(8,128)S(1)}, u32[]{:S(2)}, u32[]{:S(2)}) async-start(f32[4,288,128]{2,1,0:T(8,128)} %bitcast.45), calls=%async_computation | async-start | bytes 1179648 | tf_op jit(solution)/shard_map/x_scatter/all_to_all | solution.py:120
  74.6 9.4 %all-to-all-done = f32[4,288,128]{2,1,0:T(8,128)S(1)} async-done(((f32[4,288,128]{2,1,0:T(8,128)}), f32[4,288,128]{2,1,0:T(8,128)S(1)}, u32[]{:S(2)}, u32[]{:S(2)}) %all-to-all-start) | async-done | bytes 589856 | tf_op jit(solution)/shard_map/x_scatter/all_to_all | solution.py:120
  84.7 8.8 %all-to-all-start.1 = ((f32[8,36,128]{2,1,0:T(8,128)}), f32[8,36,128]{2,1,0:T(8,128)S(1)}, u32[]{:S(2)}, u32[]{:S(2)}) async-start(f32[8,36,128]{2,1,0:T(8,128)} %reshape.231), calls=%async_computation.1 | async-start | bytes 327680 | tf_op jit(solution)/shard_map/y_scatter/all_to_all | solution.py:123
  93.8 8.0 %all-to-all-done.1 = f32[8,36,128]{2,1,0:T(8,128)S(1)} async-done(((f32[8,36,128]{2,1,0:T(8,128)}), f32[8,36,128]{2,1,0:T(8,128)S(1)}, u32[]{:S(2)}, u32[]{:S(2)}) %all-to-all-start.1) | async-done | bytes 147488 | tf_op jit(solution)/shard_map/y_scatter/all_to_all | solution.py:123
  101.8 21.9 %all-gather.3 = f32[16,36,128]{2,1,0:T(8,128)S(1)} all-gather(f32[1,36,128]{2,1,0:T(8,128)S(1)} %bitcast.157), channel_id=2, replica_groups=mesh['x'=4,'z'=16,'core'=2,'y'=8] {'z'}, dimensions={0}, use_global_device_ids=true | all-gather | bytes 313344 | tf_op jit(solution)/shard_map/z_total/all_gather | solution.py:125
  123.8 18.6 %all-gather.4 = f32[8,36,128]{2,1,0:T(8,128)S(1)} all-gather(f32[1,36,128]{2,1,0:T(8,128)S(1)} %bitcast.156), channel_id=3, replica_groups=mesh['x'=4,'z'=16,'core'=2,'y'=8] {'y'}, dimensions={0}, use_global_device_ids=true | all-gather | bytes 165888 | tf_op jit(solution)/shard_map/y_gather/all_gather | solution.py:127
  142.3 10.3 %all-gather.2 = f32[1152,128]{1,0:T(8,128)S(1)} all-gather(f32[288,128]{1,0:T(8,128)S(1)} %reshape.244), channel_id=4, replica_groups=mesh['x'=4,'z'=16,'core'=2,'y'=8] {'x'}, dimensions={0}, use_global_device_ids=true | all-gather | bytes 737280 | tf_op jit(solution)/shard_map/x_gather/all_gather | solution.py:129
  152.6 20.4 %collective-permute-start.5 = (f32[1152,128]{1,0:T(8,128)S(1)}, f32[1152,128]{1,0:T(8,128)S(1)}, u32[]{:S(2)}, u32[]{:S(2)}) collective-permute-start(f32[1152,128]{1,0:T(8,128)S(1)} %all-gather.2), channel_id=1, source_target_pairs={{0,8},{8,0},{1,9},{9,1},{2,10},{10,2},{3,11},{11,3},{4,12},{12,4},... | collective-permute-start | bytes 1769480 | tf_op jit(solution)/shard_map/cores_back/ppermute | solution.py:131
  173.4 1.0 convolution_add_fusion.6
  174.6 1.1 broadcast_select_fusion
  (147 shorter events, 28.8 us)
Async XLA Ops:
  0.6 18.9 %copy-start.2 = (f32[3,3,128,128]{3,2,1,0:T(8,128)S(1)}, f32[3,3,128,128]{3,2,1,0:T(8,128)}, u32[]{:S(2)}) copy-start(f32[3,3,128,128]{3,2,1,0:T(8,128)} %param.6) | copy-start | bytes 1769476
  1.6 21.8 %collective-permute-start.1 = (f32[6,32,128]{2,1,0:T(8,128)S(1)}, f32[6,32,128]{2,1,0:T(8,128)S(1)}, u32[]{:S(2)}, u32[]{:S(2)}) collective-permute-start(f32[6,32,128]{2,1,0:T(8,128)S(1)} %pad_maximum_fusion.15), channel_id=1, source_target_pairs={{8,0},{16,8},{24,16},{32,24},{40,32},{48,40},{56,48},{64,56},{72,6... | collective-permute-start | bytes 294920 | tf_op jit(solution)/shard_map/ppermute | solution.py:18
  17.7 5.7 %collective-permute-start = (f32[6,32,128]{2,1,0:T(8,128)S(1)}, f32[6,32,128]{2,1,0:T(8,128)S(1)}, u32[]{:S(2)}, u32[]{:S(2)}) collective-permute-start(f32[6,32,128]{2,1,0:T(8,128)S(1)} %pad_maximum_fusion.14), channel_id=1, source_target_pairs={{0,8},{8,16},{16,24},{24,32},{32,40},{40,48},{48,56},{56,64},{64,7... | collective-permute-start | bytes 294920 | tf_op jit(solution)/shard_map/ppermute | solution.py:18
  20.4 1.1 copy-start.3
  24.8 5.4 %collective-permute-start.3 = (f32[88,128]{1,0:T(8,128)S(1)}, f32[88,128]{1,0:T(8,128)S(1)}, u32[]{:S(2)}, u32[]{:S(2)}) collective-permute-start(f32[88,128]{1,0:T(8,128)S(1)} %pad_maximum_fusion.17), channel_id=1, source_target_pairs={{1,0},{2,1},{3,2},{4,3},{5,4},{6,5},{7,6},{9,8},{10,9},{11,10},{12... | collective-permute-start | bytes 135176 | tf_op jit(solution)/shard_map/ppermute | solution.py:18
  26.1 5.1 %collective-permute-start.2 = (f32[88,128]{1,0:T(8,128)S(1)}, f32[88,128]{1,0:T(8,128)S(1)}, u32[]{:S(2)}, u32[]{:S(2)}) collective-permute-start(f32[88,128]{1,0:T(8,128)S(1)} %pad_maximum_fusion.16), channel_id=1, source_target_pairs={{0,1},{1,2},{2,3},{3,4},{4,5},{5,6},{6,7},{8,9},{9,10},{10,11},{11... | collective-permute-start | bytes 135176 | tf_op jit(solution)/shard_map/ppermute | solution.py:18
  30.2 1.0 copy-start.23
  34.9 1.0 copy-start.15
  36.0 0.9 copy-start.14
  36.5 1.2 copy-start.1
  36.9 1.0 copy-start.13
  40.0 0.9 copy-start.16
  40.9 1.5 copy-start.11
  42.4 0.9 copy-start.10
  48.1 0.9 copy-start.12
  50.0 1.0 copy-start.5
  50.0 1.1 copy-start.17
  51.5 1.0 copy-start.7
  52.5 1.0 copy-start.6
  57.8 4.4 %copy-start.4 = (f32[3,3,128,128]{3,2,1,0:T(8,128)S(1)}, f32[3,3,128,128]{3,2,1,0:T(8,128)}, u32[]{:S(2)}) copy-start(f32[3,3,128,128]{3,2,1,0:T(8,128)} %param.5) | copy-start | bytes 1769476
  58.7 5.5 %collective-permute-start.4 = (f32[1152,128]{1,0:T(8,128)}, f32[1152,128]{1,0:T(8,128)}, u32[]{:S(2)}, u32[]{:S(2)}) collective-permute-start(f32[1152,128]{1,0:T(8,128)} %multiply_select_fusion), channel_id=1, source_target_pairs={{0,8},{8,0},{1,9},{9,1},{2,10},{10,2},{3,11},{11,3},{4,12},{12,4},... | collective-permute-start | bytes 1769480 | tf_op jit(solution)/shard_map/cores/ppermute | solution.py:116
  66.2 17.8 %all-to-all-start = ((f32[4,288,128]{2,1,0:T(8,128)}), f32[4,288,128]{2,1,0:T(8,128)S(1)}, u32[]{:S(2)}, u32[]{:S(2)}) async-start(f32[4,288,128]{2,1,0:T(8,128)} %bitcast.45), calls=%async_computation | async-start | bytes 1179648 | tf_op jit(solution)/shard_map/x_scatter/all_to_all | solution.py:120
  84.7 17.1 %all-to-all-start.1 = ((f32[8,36,128]{2,1,0:T(8,128)}), f32[8,36,128]{2,1,0:T(8,128)S(1)}, u32[]{:S(2)}, u32[]{:S(2)}) async-start(f32[8,36,128]{2,1,0:T(8,128)} %reshape.231), calls=%async_computation.1 | async-start | bytes 327680 | tf_op jit(solution)/shard_map/y_scatter/all_to_all | solution.py:123
  152.6 22.0 %collective-permute-start.5 = (f32[1152,128]{1,0:T(8,128)S(1)}, f32[1152,128]{1,0:T(8,128)S(1)}, u32[]{:S(2)}, u32[]{:S(2)}) collective-permute-start(f32[1152,128]{1,0:T(8,128)S(1)} %all-gather.2), channel_id=1, source_target_pairs={{0,8},{8,0},{1,9},{9,1},{2,10},{10,2},{3,11},{11,3},{4,12},{12,4},... | collective-permute-start | bytes 1769480 | tf_op jit(solution)/shard_map/cores_back/ppermute | solution.py:131
  (11 other events, 8.6 us)

commit v2 on v1

--- a/solution.py
+++ b/solution.py
@@ -107,6 +107,11 @@
     return (row >= 0) & (row < height) & (col >= 0) & (col < width)
 
 
+def to_all(values, axis):
+    copies = jnp.broadcast_to(values[None], (lax.axis_size(axis),) + values.shape)
+    return lax.all_to_all(copies, axis, 0, 0)
+
+
 def total(first, second):
     core = lax.axis_index("core")
     other = [(0, 1), (1, 0)]
@@ -115,18 +120,13 @@
     with jax.named_scope("cores"):
         mine = mine + lax.ppermute(theirs, "core", other)
     channels = mine.shape[-1]
-    with jax.named_scope("x_scatter"):
-        n = lax.axis_size("x")
-        mine = lax.all_to_all(mine.reshape(n, -1, channels), "x", 0, 0).sum(0)
-    with jax.named_scope("y_scatter"):
-        n = lax.axis_size("y")
-        mine = lax.all_to_all(mine.reshape(n, -1, channels), "y", 0, 0).sum(0)
+    with jax.named_scope("xy_scatter"):
+        n = lax.axis_size(("x", "y"))
+        mine = lax.all_to_all(mine.reshape(n, -1, channels), ("x", "y"), 0, 0).sum(0)
     with jax.named_scope("z_total"):
-        mine = lax.all_gather(mine, "z", axis=0).sum(0)
-    with jax.named_scope("y_gather"):
-        mine = lax.all_gather(mine, "y", axis=0).reshape(-1, channels)
-    with jax.named_scope("x_gather"):
-        mine = lax.all_gather(mine, "x", axis=0).reshape(-1, channels)
+        mine = to_all(mine, "z").sum(0)
+    with jax.named_scope("xy_gather"):
+        mine = to_all(mine, ("x", "y")).reshape(-1, channels)
     with jax.named_scope("cores_back"):
         theirs = lax.ppermute(mine, "core", other)
     first = jnp.where(core == 0, theirs, mine)

time: 177 us -> 154 us (0.87)
  starting transfers between devices: 64.2 us -> 47.8 us
  waiting for transfers between devices: 20.4 us -> 15.5 us
  other arithmetic: 9.04 us -> 6.74 us
    all_gather x3 -> x0, blocking collectives: 50.7 us -> none  [the longest x1 21.9 us: total(): mine = lax.all_gather(mine, 'z', axis=0).sum(0)]
    all_to_all x0 -> x2, blocking collectives: none -> 49.2 us  [the longest x1 33.1 us: total(): lax.all_to_all(mine.reshape(n, -1, channels), ('x', 'y'), 0, 0).sum(0)]
    ppermute x1, starting transfers between devices: 20.4 us -> 10.7 us  [total(): theirs = lax.ppermute(mine, 'core', other)]
    all_to_all x2 -> x1, starting transfers between devices: 17 us -> 10.3 us  [to_all(): return lax.all_to_all(copies, axis, 0, 0)]
    all_to_all x2 -> x1, waiting for transfers between devices: 17.4 us -> 12.6 us  [to_all(): return lax.all_to_all(copies, axis, 0, 0)]
    add x1, other arithmetic: 1.96 us -> 0.08 us  [total(): mine = mine + lax.ppermute(theirs, 'core', other)]
    unnamed x53 -> x60, local copies, waits for them, and re-layouts: 8.54 us -> 8.88 us
  transfers between devices with their start and end apart: 8 -> 7, of which waited for: 5 -> 4; matrix products, arithmetic and copies ran while one was open for 3% -> 3% of each run, Pallas kernels for 0% -> 0%
where the time goes in v2:
time: 154 us; the launch traced here: 151 us
  blocking collectives  49.2 us (32%)
  starting transfers between devices  47.8 us (31%)
  local copies, waits for them, and re-layouts  18.8 us (12%)
  waiting for transfers between devices  15.5 us (10%)
  matrix products  11.9 us (8%)
  other arithmetic  6.74 us (4%)
    all_to_all x1, blocking collectives, total(): lax.all_to_all(mine.reshape(n, -1, channels), ('x', 'y'), 0, 0).sum(0)  33.1 us
    ppermute x2, starting transfers between devices, neighbours(): lax.ppermute(high, axis, backward)  17.4 us
    all_to_all x1, blocking collectives, to_all(): return lax.all_to_all(copies, axis, 0, 0)  16.1 us
    all_to_all x1, waiting for transfers between devices, to_all(): return lax.all_to_all(copies, axis, 0, 0)  12.6 us
    ppermute x1, starting transfers between devices, total(): theirs = lax.ppermute(mine, 'core', other)  10.7 us
    all_to_all x1, starting transfers between devices, to_all(): return lax.all_to_all(copies, axis, 0, 0)  10.3 us
    unnamed x60, local copies, waits for them, and re-layouts  8.88 us
    dot_general x12, matrix products, shifted_product(): jnp.dot(stacked.reshape(out_rows * out_cols, -1), kernel[row_shift].resha...  6.77 us
  transfers between devices with their start and end apart: 7, of which 4 were waited for; matrix products, arithmetic and copies ran while one was open for 3% of the time, Pallas kernels for 0%

profile of v2, /device:TPU:1, one launch (start us, length us, event | category | flops | bytes accessed | tf_op | source)
XLA Modules:
  0.0 151.4 jit_solution(1191710243775630606)
XLA Ops:
  1.6 16.1 %collective-permute-start.1 = (f32[6,32,128]{2,1,0:T(8,128)S(1)}, f32[6,32,128]{2,1,0:T(8,128)S(1)}, u32[]{:S(2)}, u32[]{:S(2)}) collective-permute-start(f32[6,32,128]{2,1,0:T(8,128)S(1)} %pad_maximum_fusion.15), channel_id=1, source_target_pairs={{8,0},{16,8},{24,16},{32,24},{40,32},{48,40},{56,48},{64,56},{72,6... | collective-permute-start | bytes 294920 | tf_op jit(solution)/shard_map/ppermute | solution.py:18
  17.7 1.9 %collective-permute-start = (f32[6,32,128]{2,1,0:T(8,128)S(1)}, f32[6,32,128]{2,1,0:T(8,128)S(1)}, u32[]{:S(2)}, u32[]{:S(2)}) collective-permute-start(f32[6,32,128]{2,1,0:T(8,128)S(1)} %pad_maximum_fusion.14), channel_id=1, source_target_pairs={{0,8},{8,16},{16,24},{24,32},{32,40},{40,48},{48,56},{56,64},{64,7... | collective-permute-start | bytes 294920 | tf_op jit(solution)/shard_map/ppermute | solution.py:18
  24.2 1.3 collective-permute-start.3
  25.5 4.0 %collective-permute-start.2 = (f32[88,128]{1,0:T(8,128)S(1)}, f32[88,128]{1,0:T(8,128)S(1)}, u32[]{:S(2)}, u32[]{:S(2)}) collective-permute-start(f32[88,128]{1,0:T(8,128)S(1)} %pad_maximum_fusion.16), channel_id=1, source_target_pairs={{0,1},{1,2},{2,3},{3,4},{4,5},{5,6},{6,7},{8,9},{9,10},{10,11},{11... | collective-permute-start | bytes 135176 | tf_op jit(solution)/shard_map/ppermute | solution.py:18
  29.6 1.0 collective-permute-done.2
  31.3 0.9 pad_maximum_fusion.13
  32.2 1.0 fusion.67
  34.6 1.0 reshape.212
  38.2 0.9 fusion.68
  39.4 1.2 pad_maximum_fusion.5
  40.7 1.4 fusion.74
  44.5 1.0 fusion.69
  45.9 1.2 pad_maximum_fusion.7
  47.2 1.1 pad_maximum_fusion.8
  58.7 3.5 %collective-permute-start.4 = (f32[1152,128]{1,0:T(8,128)S(1)}, f32[1152,128]{1,0:T(8,128)S(1)}, u32[]{:S(2)}, u32[]{:S(2)}) collective-permute-start(f32[1152,128]{1,0:T(8,128)S(1)} %multiply_select_fusion), channel_id=1, source_target_pairs={{0,8},{8,0},{1,9},{9,1},{2,10},{10,2},{3,11},{11,3},{4,12},{12,4},... | collective-permute-start | bytes 1769480 | tf_op jit(solution)/shard_map/cores/ppermute | solution.py:121
  62.3 1.6 %collective-permute-done.4 = f32[1152,128]{1,0:T(8,128)S(1)} collective-permute-done((f32[1152,128]{1,0:T(8,128)S(1)}, f32[1152,128]{1,0:T(8,128)S(1)}, u32[]{:S(2)}, u32[]{:S(2)}) %collective-permute-start.4) | collective-permute-done | bytes 589856 | tf_op jit(solution)/shard_map/cores/ppermute | solution.py:121
  64.0 33.1 %all_to_all.15 = f32[32,36,128]{2,1,0:T(8,128)S(1)} all-to-all(f32[32,36,128]{2,1,0:T(8,128)S(1)} %reshape.226), channel_id=1, replica_groups=mesh['x'=4,'z'=16,'core'=2,'y'=8] {'x','y'}, dimensions={0} | all-to-all | bytes 1179648 | tf_op jit(solution)/shard_map/xy_scatter/all_to_all | solution.py:125
  97.2 16.1 %all_to_all.16 = f32[16,36,128]{2,1,0:T(8,128)S(1)} all-to-all(f32[16,36,128]{2,1,0:T(8,128)S(1)} %broadcast_in_dim.40), channel_id=1, replica_groups=mesh['x'=4,'z'=16,'core'=2,'y'=8] {'z'}, dimensions={0} | all-to-all | bytes 589824 | tf_op jit(solution)/shard_map/z_total/all_to_all | solution.py:112
  113.3 0.9 broadcast_in_dim.41
  114.2 10.3 %all-to-all-start.2 = ((f32[32,36,128]{2,1,0:T(8,128)}), f32[32,36,128]{2,1,0:T(8,128)S(1)}, u32[]{:S(2)}, u32[]{:S(2)}) async-start(f32[32,36,128]{2,1,0:T(8,128)} %broadcast_in_dim.41), calls=%async_computation.2 | async-start | bytes 1310720 | tf_op jit(solution)/shard_map/xy_gather/all_to_all | solution.py:112
  125.4 12.6 %all-to-all-done.2 = f32[32,36,128]{2,1,0:T(8,128)S(1)} async-done(((f32[32,36,128]{2,1,0:T(8,128)}), f32[32,36,128]{2,1,0:T(8,128)S(1)}, u32[]{:S(2)}, u32[]{:S(2)}) %all-to-all-start.2) | async-done | bytes 589856 | tf_op jit(solution)/shard_map/xy_gather/all_to_all | solution.py:112
  138.0 10.7 %collective-permute-start.5 = (f32[1152,128]{1,0:T(8,128)S(1)}, f32[1152,128]{1,0:T(8,128)S(1)}, u32[]{:S(2)}, u32[]{:S(2)}) collective-permute-start(f32[1152,128]{1,0:T(8,128)S(1)} %reshape.227), channel_id=1, source_target_pairs={{0,8},{8,0},{1,9},{9,1},{2,10},{10,2},{3,11},{11,3},{4,12},{12,4},... | collective-permute-start | bytes 1769480 | tf_op jit(solution)/shard_map/cores_back/ppermute | solution.py:131
  149.1 1.0 convolution_add_fusion.6
  150.3 1.1 broadcast_select_fusion
  (153 shorter events, 25.2 us)
Async XLA Ops:
  0.6 18.9 %copy-start.2 = (f32[3,3,128,128]{3,2,1,0:T(8,128)S(1)}, f32[3,3,128,128]{3,2,1,0:T(8,128)}, u32[]{:S(2)}) copy-start(f32[3,3,128,128]{3,2,1,0:T(8,128)} %param.6) | copy-start | bytes 1769476
  1.6 21.8 %collective-permute-start.1 = (f32[6,32,128]{2,1,0:T(8,128)S(1)}, f32[6,32,128]{2,1,0:T(8,128)S(1)}, u32[]{:S(2)}, u32[]{:S(2)}) collective-permute-start(f32[6,32,128]{2,1,0:T(8,128)S(1)} %pad_maximum_fusion.15), channel_id=1, source_target_pairs={{8,0},{16,8},{24,16},{32,24},{40,32},{48,40},{56,48},{64,56},{72,6... | collective-permute-start | bytes 294920 | tf_op jit(solution)/shard_map/ppermute | solution.py:18
  17.7 5.7 %collective-permute-start = (f32[6,32,128]{2,1,0:T(8,128)S(1)}, f32[6,32,128]{2,1,0:T(8,128)S(1)}, u32[]{:S(2)}, u32[]{:S(2)}) collective-permute-start(f32[6,32,128]{2,1,0:T(8,128)S(1)} %pad_maximum_fusion.14), channel_id=1, source_target_pairs={{0,8},{8,16},{16,24},{24,32},{32,40},{40,48},{48,56},{56,64},{64,7... | collective-permute-start | bytes 294920 | tf_op jit(solution)/shard_map/ppermute | solution.py:18
  20.4 1.1 copy-start.3
  24.2 6.6 %copy-start.6 = (f32[4,32,128]{2,1,0:T(8,128)}, f32[4,32,128]{2,1,0:T(8,128)S(1)}, u32[]{:S(2)}) copy-start(f32[4,32,128]{2,1,0:T(8,128)S(1)} %slice.414) | copy-start | bytes 196612
  24.2 6.5 %copy-start.8 = (f32[4,32,128]{2,1,0:T(8,128)}, f32[4,32,128]{2,1,0:T(8,128)S(1)}, u32[]{:S(2)}) copy-start(f32[4,32,128]{2,1,0:T(8,128)S(1)} %slice.413) | copy-start | bytes 196612
  24.2 5.4 %collective-permute-start.3 = (f32[88,128]{1,0:T(8,128)S(1)}, f32[88,128]{1,0:T(8,128)S(1)}, u32[]{:S(2)}, u32[]{:S(2)}) collective-permute-start(f32[88,128]{1,0:T(8,128)S(1)} %pad_maximum_fusion.17), channel_id=1, source_target_pairs={{1,0},{2,1},{3,2},{4,3},{5,4},{6,5},{7,6},{9,8},{10,9},{11,10},{12... | collective-permute-start | bytes 135176 | tf_op jit(solution)/shard_map/ppermute | solution.py:18
  25.5 5.1 %collective-permute-start.2 = (f32[88,128]{1,0:T(8,128)S(1)}, f32[88,128]{1,0:T(8,128)S(1)}, u32[]{:S(2)}, u32[]{:S(2)}) collective-permute-start(f32[88,128]{1,0:T(8,128)S(1)} %pad_maximum_fusion.16), channel_id=1, source_target_pairs={{0,1},{1,2},{2,3},{3,4},{4,5},{5,6},{6,7},{8,9},{9,10},{10,11},{11... | collective-permute-start | bytes 135176 | tf_op jit(solution)/shard_map/ppermute | solution.py:18
  29.6 1.0 copy-start.27
  33.3 1.0 copy-start.12
  33.4 1.0 copy-start.13
  33.4 1.1 copy-start.14
  34.5 1.0 copy-start.22
  36.1 1.2 copy-start.1
  36.5 1.0 copy-start.20
  40.7 1.4 copy-start.18
  50.1 1.0 copy-start.5
  50.1 1.1 copy-start.23
  51.6 1.0 copy-start.11
  52.6 1.1 copy-start.10
  58.7 5.2 %collective-permute-start.4 = (f32[1152,128]{1,0:T(8,128)S(1)}, f32[1152,128]{1,0:T(8,128)S(1)}, u32[]{:S(2)}, u32[]{:S(2)}) collective-permute-start(f32[1152,128]{1,0:T(8,128)S(1)} %multiply_select_fusion), channel_id=1, source_target_pairs={{0,8},{8,0},{1,9},{9,1},{2,10},{10,2},{3,11},{11,3},{4,12},{12,4},... | collective-permute-start | bytes 1769480 | tf_op jit(solution)/shard_map/cores/ppermute | solution.py:121
  114.2 10.3 %copy-start.4 = (f32[3,3,128,128]{3,2,1,0:T(8,128)S(1)}, f32[3,3,128,128]{3,2,1,0:T(8,128)}, u32[]{:S(2)}) copy-start(f32[3,3,128,128]{3,2,1,0:T(8,128)} %param.5) | copy-start | bytes 1769476
  114.2 23.7 %all-to-all-start.2 = ((f32[32,36,128]{2,1,0:T(8,128)}), f32[32,36,128]{2,1,0:T(8,128)S(1)}, u32[]{:S(2)}, u32[]{:S(2)}) async-start(f32[32,36,128]{2,1,0:T(8,128)} %broadcast_in_dim.41), calls=%async_computation.2 | async-start | bytes 1310720 | tf_op jit(solution)/shard_map/xy_gather/all_to_all | solution.py:112
  138.0 12.3 %collective-permute-start.5 = (f32[1152,128]{1,0:T(8,128)S(1)}, f32[1152,128]{1,0:T(8,128)S(1)}, u32[]{:S(2)}, u32[]{:S(2)}) collective-permute-start(f32[1152,128]{1,0:T(8,128)S(1)} %reshape.227), channel_id=1, source_target_pairs={{0,8},{8,0},{1,9},{9,1},{2,10},{10,2},{3,11},{11,3},{4,12},{12,4},... | collective-permute-start | bytes 1769480 | tf_op jit(solution)/shard_map/cores_back/ppermute | solution.py:131
  (14 other events, 12.0 us)

commit v3 on v2

v3 whole, which is shorter than its diff:
```python
import functools
import math

import jax
import jax.numpy as jnp
from jax import lax
from jax.experimental import pallas as pl
from jax.experimental.pallas import tpu as pltpu
from jax.sharding import Mesh, PartitionSpec as P

ROWS = ("x", "z", "core")
FIELD_HALO = 4
COT_HALO = 2
PITCH = 48
LEFT = 8
SLACK = 8
VMEM_LIMIT = 40 * 2**20
PARAMS = pltpu.CompilerParams(vmem_limit_bytes=VMEM_LIMIT)
IN_VMEM = pl.BlockSpec(memory_space=pltpu.VMEM)
IN_SMEM = pl.BlockSpec(memory_space=pltpu.SMEM)


def neighbours(values, axis):
    count = lax.axis_size(axis)
    forward = [(i, i + 1) for i in range(count - 1)]
    backward = [(target, source) for source, target in forward]
    low, high = values
    return lax.ppermute(low, axis, forward), lax.ppermute(high, axis, backward)


def image(rows, dtype=jnp.float32):
    return pltpu.VMEM((2 * SLACK + rows * PITCH, 128), dtype)


def spot(row, col):
    return SLACK + row * PITCH + col


def pack_kernel(field, cot, low, high, to_low, to_high):
    a, b = FIELD_HALO, COT_HALO
    tile_rows, tile_cols, _ = field.shape
    for out, col_a, col_b in ((to_low, 0, 0), (to_high, tile_cols - a, tile_cols - b)):
        at = 0
        for part, rows, col, count in (
            (low, range(a), col_a, a),
            (field, range(tile_rows), col_a, a),
            (high, range(a), col_a, a),
            (low, range(a, a + b), col_b, b),
            (cot, range(tile_rows), col_b, b),
            (high, range(a, a + b), col_b, b),
        ):
            for row in rows:
                out[at : at + count, :] = part[row, col : col + count, :]
                at += count


def split(values):
    high = values.astype(jnp.bfloat16)
    low = (values - high.astype(jnp.float32)).astype(jnp.bfloat16)
    return high, low


def load_filter(source, flip, both, first):
    for a in range(3):
        if flip:
            taps = jnp.concatenate([source[2 - a, 2 - b] for b in range(3)], axis=1)
        else:
            taps = source[a].reshape(-1, source.shape[3])
        high, low = split(taps)
        both[a] = jnp.concatenate([high, low], axis=0 if flip else 1)
        first[a] = high


def convolve(source, rows, flip, both, first, high, low):
    taken = (rows + 2) * PITCH
    made = rows * PITCH
    shifts = [source[SLACK - 1 + b : SLACK - 1 + b + taken, :] for b in range(3)]
    for b in range(3):
        part_high, part_low = split(shifts[b])
        high[0:taken, 128 * b : 128 * b + 128] = part_high
        low[0:taken, 128 * b : 128 * b + 128] = part_low
    dims = (((1,), (1 if flip else 0,)), ((), ()))
    wide = None
    thin = None
    for a in range(3):
        start = a * PITCH
        p = lax.dot_general(
            high[start : start + made, :], both[a], dims, preferred_element_type=jnp.float32
        )
        q = lax.dot_general(
            low[start : start + made, :], first[a], dims, preferred_element_type=jnp.float32
        )
        wide = p if wide is None else wide + p
        thin = q if thin is None else thin + q
    return wide[:, :128] + wide[:, 128:] + thin


def filter_product(values, value_row, deltas, delta_row, tile_rows, tile_cols, factor):
    rows = tile_rows + 2
    windows = []
    for b in range(3):
        col = LEFT - 1 + b
        windows.append(
            jnp.concatenate(
                [
                    values[spot(value_row + r, col) : spot(value_row + r, col) + tile_cols, :]
                    for r in range(rows)
                ],
                axis=0,
            )
        )
    high, low = split(jnp.concatenate(windows, axis=1))
    delta = jnp.concatenate(
        [
            deltas[spot(delta_row + r, LEFT) : spot(delta_row + r, LEFT) + tile_cols, :]
            for r in range(tile_rows)
        ],
        axis=0,
    )
    delta_high, delta_low = split((delta * factor).T)
    pixels = tile_rows * tile_cols
    outs = []
    for a in range(3):
        start = a * tile_cols
        window = high[start : start + pixels]
        out = jnp.dot(delta_high, window, preferred_element_type=jnp.float32)
        out += jnp.dot(
            delta_high, low[start : start + pixels], preferred_element_type=jnp.float32
        )
        out += jnp.dot(delta_low, window, preferred_element_type=jnp.float32)
        outs.append(out.T)
    return jnp.concatenate(outs, axis=0)


def inside(place, rows, margin, tile_rows, tile_cols, height, width):
    shape = (rows, PITCH, 128)
    row = lax.broadcasted_iota(jnp.int32, shape, 0) + (place[0] * tile_rows - margin)
    col = lax.broadcasted_iota(jnp.int32, shape, 1) + (place[1] * tile_cols - LEFT)
    keep = (row >= 0) & (row < height) & (col >= 0) & (col < width)
    return jnp.where(keep, 1.0, 0.0).reshape(rows * PITCH, 128) > 0.5


def main_kernel(
    height, width, place, field, cot, low, high, from_low, from_high, filter_first, filter_second,
    kept, sent, first_delta_out,
    field_image, cot_image, hidden_image, slope_image, delta_image,
    both, first, both_back, first_back, part_high, part_low,
):
    a, b = FIELD_HALO, COT_HALO
    tile_rows, tile_cols, _ = field.shape
    for target, own, halo, base, offset in (
        (field_image, field, a, 0, 0),
        (cot_image, cot, b, a, (tile_rows + 2 * a) * a),
    ):
        for row in range(tile_rows + 2 * halo):
            if row < halo:
                line = low[base + row]
            elif row < halo + tile_rows:
                line = own[row - halo]
            else:
                line = high[base + row - halo - tile_rows]
            target[spot(row, LEFT) : spot(row, LEFT) + tile_cols, :] = line
            left = spot(row, LEFT - halo)
            target[left : left + halo, :] = from_low[offset + row * halo : offset + row * halo + halo, :]
            right = spot(row, LEFT + tile_cols)
            target[right : right + halo, :] = from_high[
                offset + row * halo : offset + row * halo + halo, :
            ]
    grid = (tile_rows, tile_cols, height, width)
    factor = 1.0 / math.sqrt(height * width)
    core = place[2]

    rows = tile_rows + 6
    load_filter(filter_first, False, both.at[0], first.at[0])
    pre = convolve(field_image, rows, False, both.at[0], first.at[0], part_high, part_low)
    sigmoid = jax.nn.sigmoid(pre)
    slope_image[SLACK : SLACK + rows * PITCH, :] = sigmoid * (1.0 + pre * (1.0 - sigmoid))
    hidden_image[SLACK : SLACK + rows * PITCH, :] = jnp.where(
        inside(place, rows, 3, *grid), pre * sigmoid, 0.0
    )

    rows = tile_rows + 4
    load_filter(filter_second, False, both.at[1], first.at[1])
    pre = convolve(hidden_image, rows, False, both.at[1], first.at[1], part_high, part_low)
    sigmoid = jax.nn.sigmoid(pre)
    delta_image[SLACK : SLACK + rows * PITCH, :] = cot_image[SLACK : SLACK + rows * PITCH, :] * (
        sigmoid * (1.0 + pre * (1.0 - sigmoid))
    )
    grad = filter_product(hidden_image, 2, delta_image, 2, tile_rows, tile_cols, factor)

    @pl.when(core == 0)
    def _():
        kept[...] = grad

    @pl.when(core != 0)
    def _():
        sent[...] = grad

    rows = tile_rows + 2
    load_filter(filter_second, True, both_back, first_back)
    back = convolve(delta_image, rows, True, both_back, first_back, part_high, part_low)
    start = spot(2, 0)
    first_delta_out[SLACK : SLACK + rows * PITCH, :] = jnp.where(
        inside(place, rows, 1, *grid), back * slope_image[start : start + rows * PITCH, :], 0.0
    )
    grad = filter_product(field_image, 3, first_delta_out, 1, tile_rows, tile_cols, factor)

    @pl.when(core == 0)
    def _():
        sent[...] = grad

    @pl.when(core != 0)
    def _():
        kept[...] = grad


def input_kernel(first_delta, filter_first, input_grad, both_back, first_back, part_high, part_low):
    tile_rows, tile_cols, _ = input_grad.shape
    load_filter(filter_first, True, both_back, first_back)
    out = convolve(first_delta, tile_rows, True, both_back, first_back, part_high, part_low)
    for row in range(tile_rows):
        start = row * PITCH + LEFT
        input_grad[row] = out[start : start + tile_cols]


def filters_scratch(flip):
    if flip:
        return [pltpu.VMEM((3, 256, 384), jnp.bfloat16), pltpu.VMEM((3, 128, 384), jnp.bfloat16)]
    return [pltpu.VMEM((2, 3, 384, 256), jnp.bfloat16), pltpu.VMEM((2, 3, 384, 128), jnp.bfloat16)]


def parts_scratch(rows):
    return [pltpu.VMEM((rows * PITCH, 384), jnp.bfloat16)] * 2


def to_all(values, axis):
    copies = jnp.broadcast_to(values[None], (lax.axis_size(axis),) + values.shape)
    return lax.all_to_all(copies, axis, 0, 0)


def total(mine, theirs):
    core = lax.axis_index("core")
    other = [(0, 1), (1, 0)]
    with jax.named_scope("cores"):
        mine = mine + lax.ppermute(theirs, "core", other)
    channels = mine.shape[-1]
    with jax.named_scope("xy_scatter"):
        n = lax.axis_size(("x", "y"))
        mine = lax.all_to_all(mine.reshape(n, -1, channels), ("x", "y"), 0, 0).sum(0)
    with jax.named_scope("z_total"):
        mine = to_all(mine, "z").sum(0)
    with jax.named_scope("xy_gather"):
        mine = to_all(mine, ("x", "y")).reshape(-1, channels)
    with jax.named_scope("cores_back"):
        theirs = lax.ppermute(mine, "core", other)
    first = jnp.where(core == 0, theirs, mine)
    second = jnp.where(core == 0, mine, theirs)
    return first, second


def local(field, filter_first, filter_second, cotangent):
    tile_rows, tile_cols, channels = field.shape
    a, b = FIELD_HALO, COT_HALO
    height = tile_rows * lax.axis_size(ROWS)
    width = tile_cols * lax.axis_size("y")
    place = jnp.stack([lax.axis_index(ROWS), lax.axis_index("y"), lax.axis_index("core")])
    place = place.astype(jnp.int32)
    low, high = neighbours(
        (
            jnp.concatenate([field[-a:], cotangent[-b:]], axis=0),
            jnp.concatenate([field[:a], cotangent[:b]], axis=0),
        ),
        ROWS,
    )
    lines = (tile_rows + 2 * a) * a + (tile_rows + 2 * b) * b
    side = jax.ShapeDtypeStruct((lines, channels), jnp.float32)
    to_low, to_high = pl.pallas_call(
        pack_kernel,
        out_shape=(side, side),
        in_specs=[IN_VMEM] * 4,
        out_specs=(IN_VMEM, IN_VMEM),
        compiler_params=PARAMS,
        name="pack_sides",
    )(field, cotangent, low, high)
    from_low, from_high = neighbours((to_high, to_low), "y")
    grad = jax.ShapeDtypeStruct((9 * channels, channels), jnp.float32)
    delta_rows = tile_rows + 2
    kept, sent, first_delta = pl.pallas_call(
        functools.partial(main_kernel, height, width),
        out_shape=(
            grad,
            grad,
            jax.ShapeDtypeStruct((2 * SLACK + delta_rows * PITCH, channels), jnp.float32),
        ),
        in_specs=[IN_SMEM] + [IN_VMEM] * 8,
        out_specs=(IN_VMEM, IN_VMEM, IN_VMEM),
        scratch_shapes=[
            image(tile_rows + 2 * a),
            image(tile_rows + 2 * b),
            image(tile_rows + 6),
            image(tile_rows + 6),
            image(tile_rows + 4),
            *filters_scratch(False),
            *filters_scratch(True),
            *parts_scratch(tile_rows + 2 * a),
        ],
        compiler_params=PARAMS,
        name="gradients",
    )(place, field, cotangent, low, high, from_low, from_high, filter_first, filter_second)
    first_grad, second_grad = total(kept, sent)
    input_grad = pl.pallas_call(
        input_kernel,
        out_shape=jax.ShapeDtypeStruct(field.shape, jnp.float32),
        in_specs=[IN_VMEM] * 2,
        out_specs=IN_VMEM,
        scratch_shapes=[*filters_scratch(True), *parts_scratch(delta_rows)],
        compiler_params=PARAMS,
        cost_estimate=pl.CostEstimate(flops=2 * 10**9, bytes_accessed=10**6, transcendentals=0),
        name="input_grad",
    )(first_delta, filter_first)
    shape = filter_first.shape
    return (input_grad, first_grad.reshape(shape), second_grad.reshape(shape))


def solution(mesh):
    fine = Mesh(mesh.devices.reshape(4, 16, 2, 8), ("x", "z", "core", "y"))
    tile = P(ROWS, "y", None)
    return jax.shard_map(
        local, mesh=fine, in_specs=(tile, P(), P(), tile), out_specs=(tile, P(), P()), check_vma=False
    )
```

time: 154 us -> 131 us (0.85)
  the two profiles are of different devices: /device:TPU:1 before, /device:TPU:73 now
where the time goes in v3:
time: 131 us; the launch traced here: 130 us
  blocking collectives  89.5 us (68%)
  starting transfers between devices  19.9 us (15%)
  waiting for transfers between devices  8.79 us (7%)
  Pallas kernels  6.87 us (5%)
  local copies, waits for them, and re-layouts  3.23 us (2%)
  other arithmetic  1.33 us (1%)
    all_to_all x2, blocking collectives, to_all(): return lax.all_to_all(copies, axis, 0, 0)  60.2 us
    all_to_all x1, blocking collectives, total(): lax.all_to_all(mine.reshape(n, -1, channels), ('x', 'y'), 0, 0).sum(0)  29.2 us
    ppermute x2, starting transfers between devices, neighbours(): lax.ppermute(low, axis, forward)  7.9 us
    ppermute x2, waiting for transfers between devices, neighbours(): lax.ppermute(high, axis, backward)  6.61 us
    ppermute x1, starting transfers between devices, total(): theirs = lax.ppermute(mine, 'core', other)  6.1 us
    pallas_call x1, Pallas kernels, local(): pl.pallas_call(functools.partial(main_kernel, height, width), out_shape=(...  5.46 us
    ppermute x2, starting transfers between devices, neighbours(): lax.ppermute(high, axis, backward)  4 us
  transfers between devices with their start and end apart: 6, of which 4 were waited for; matrix products, arithmetic and copies ran while one was open for 0% of the time, Pallas kernels for 1%

profile of v3, /device:TPU:73, one launch (start us, length us, event | category | flops | bytes accessed | tf_op | source)
XLA Modules:
  0.0 130.4 jit_solution(109019781640664071)
XLA Ops:
  0.6 0.8 fusion.1
  1.5 0.1 copy-done
  1.6 0.0 copy-start.1
  1.6 4.7 %collective-permute-start = (f32[6,32,128]{2,1,0:T(8,128)S(1)}, f32[6,32,128]{2,1,0:T(8,128)S(1)}, u32[]{:S(2)}, u32[]{:S(2)}) collective-permute-start(f32[6,32,128]{2,1,0:T(8,128)S(1)} %pad_maximum_fusion), channel_id=1, source_target_pairs={{0,8},{8,16},{16,24},{24,32},{32,40},{40,48},{48,56},{56,64},{64,7... | collective-permute-start | bytes 294920 | tf_op jit(solution)/shard_map/ppermute | solution.py:28
  6.3 1.9 %collective-permute-start.1 = (f32[6,32,128]{2,1,0:T(8,128)S(1)}, f32[6,32,128]{2,1,0:T(8,128)S(1)}, u32[]{:S(2)}, u32[]{:S(2)}) collective-permute-start(f32[6,32,128]{2,1,0:T(8,128)S(1)} %pad_maximum_fusion.1), channel_id=1, source_target_pairs={{8,0},{16,8},{24,16},{32,24},{40,32},{48,40},{56,48},{64,56},{72,6... | collective-permute-start | bytes 294920 | tf_op jit(solution)/shard_map/ppermute | solution.py:28
  8.3 4.0 %collective-permute-done.1.high = f32[6,32,128]{2,1,0:T(8,128)S(1)} collective-permute-done((f32[6,32,128]{2,1,0:T(8,128)S(1)}, f32[6,32,128]{2,1,0:T(8,128)S(1)}, u32[]{:S(2)}, u32[]{:S(2)}) %collective-permute-start.1) | collective-permute-done | bytes 98336 | tf_op jit(solution)/shard_map/ppermute | solution.py:28
  12.3 3.2 %collective-permute-start.2 = (f32[88,128]{1,0:T(8,128)S(1)}, f32[88,128]{1,0:T(8,128)S(1)}, u32[]{:S(2)}, u32[]{:S(2)}) collective-permute-start(f32[88,128]{1,0:T(8,128)S(1)} %get-tuple-element.8), channel_id=1, source_target_pairs={{0,1},{1,2},{2,3},{3,4},{4,5},{5,6},{6,7},{8,9},{9,10},{10,11},{11... | collective-permute-start | bytes 135176 | tf_op jit(solution)/shard_map/ppermute | solution.py:28
  15.5 2.1 %collective-permute-start.3 = (f32[88,128]{1,0:T(8,128)S(1)}, f32[88,128]{1,0:T(8,128)S(1)}, u32[]{:S(2)}, u32[]{:S(2)}) collective-permute-start(f32[88,128]{1,0:T(8,128)S(1)} %get-tuple-element.9), channel_id=1, source_target_pairs={{1,0},{2,1},{3,2},{4,3},{5,4},{6,5},{7,6},{9,8},{10,9},{11,10},{12... | collective-permute-start | bytes 135176 | tf_op jit(solution)/shard_map/ppermute | solution.py:28
  17.6 0.1 pad_add_fusion.place
  17.7 2.6 %collective-permute-done.3.from_high = f32[88,128]{1,0:T(8,128)S(1)} collective-permute-done((f32[88,128]{1,0:T(8,128)S(1)}, f32[88,128]{1,0:T(8,128)S(1)}, u32[]{:S(2)}, u32[]{:S(2)}) %collective-permute-start.3) | collective-permute-done | bytes 45088 | tf_op jit(solution)/shard_map/ppermute | solution.py:28
  20.3 1.1 copy-done.2
  21.4 1.1 copy-done.3
  22.4 5.5 %gradients.1 = (f32[1152,128]{1,0:T(8,128)S(1)}, f32[1152,128]{1,0:T(8,128)S(1)}, f32[496,128]{1,0:T(8,128)S(1)}) custom-call(s32[3]{0:T(128)S(1)} %pad_add_fusion.place, f32[8,32,128]{2,1,0:T(8,128)S(1)} %copy-done, f32[8,32,128]{2,1,0:T(8,128)S(1)} %copy-done.1, f32[6,32,128]{2,1,0:T(8,128)S(1)} %collective-permute-done.low, ...), custom_call_target="tpu_custom_call" | custom-call | tf_op jit(solution)/shard_map/gradients/pallas_call | solution.py:288
  27.9 1.9 %collective-permute-start.4 = (f32[1152,128]{1,0:T(8,128)S(1)}, f32[1152,128]{1,0:T(8,128)S(1)}, u32[]{:S(2)}, u32[]{:S(2)}) collective-permute-start(f32[1152,128]{1,0:T(8,128)S(1)} %get-tuple-element.12), channel_id=1, source_target_pairs={{0,8},{8,0},{1,9},{9,1},{2,10},{10,2},{3,11},{11,3},{4,12},{12,4},... | collective-permute-start | bytes 1769480 | tf_op jit(solution)/shard_map/cores/ppermute | solution.py:245
  29.8 2.0 %collective-permute-done.4 = f32[1152,128]{1,0:T(8,128)S(1)} collective-permute-done((f32[1152,128]{1,0:T(8,128)S(1)}, f32[1152,128]{1,0:T(8,128)S(1)}, u32[]{:S(2)}, u32[]{:S(2)}) %collective-permute-start.4) | collective-permute-done | bytes 589856 | tf_op jit(solution)/shard_map/cores/ppermute | solution.py:245
  31.8 0.1 add.11
  31.9 29.2 %all_to_all.15 = f32[32,36,128]{2,1,0:T(8,128)S(1)} all-to-all(f32[32,36,128]{2,1,0:T(8,128)S(1)} %reshape.20), channel_id=1, replica_groups=mesh['x'=4,'z'=16,'core'=2,'y'=8] {'x','y'}, dimensions={0} | all-to-all | bytes 1179648 | tf_op jit(solution)/shard_map/xy_scatter/all_to_all | solution.py:249
  61.2 0.1 reduce_sum.18
  61.2 36.5 %all_to_all.16 = f32[16,36,128]{2,1,0:T(8,128)S(1)} all-to-all(f32[16,36,128]{2,1,0:T(8,128)S(1)} %broadcast_in_dim.4), channel_id=1, replica_groups=mesh['x'=4,'z'=16,'core'=2,'y'=8] {'z'}, dimensions={0} | all-to-all | bytes 589824 | tf_op jit(solution)/shard_map/z_total/all_to_all | solution.py:238
  97.9 23.7 %all_to_all.17 = f32[32,36,128]{2,1,0:T(8,128)S(1)} all-to-all(f32[32,36,128]{2,1,0:T(8,128)S(1)} %broadcast_in_dim.5), channel_id=1, replica_groups=mesh['x'=4,'z'=16,'core'=2,'y'=8] {'x','y'}, dimensions={0} | all-to-all | bytes 1179648 | tf_op jit(solution)/shard_map/xy_gather/all_to_all | solution.py:238
  121.6 6.1 %collective-permute-start.5 = (f32[1152,128]{1,0:T(8,128)S(1)}, f32[1152,128]{1,0:T(8,128)S(1)}, u32[]{:S(2)}, u32[]{:S(2)}) collective-permute-start(f32[1152,128]{1,0:T(8,128)S(1)} %reshape.21), channel_id=1, source_target_pairs={{0,8},{8,0},{1,9},{9,1},{2,10},{10,2},{3,11},{11,3},{4,12},{12,4},... | collective-permute-start | bytes 1769480 | tf_op jit(solution)/shard_map/cores_back/ppermute | solution.py:255
  127.7 1.4 %input_grad.1 = f32[8,32,128]{2,1,0:T(8,128)} custom-call(f32[496,128]{1,0:T(8,128)S(1)} %get-tuple-element.10.first_delta, f32[3,3,128,128]{3,2,1,0:T(8,128)S(1)} %copy-done.4), custom_call_target="tpu_custom_call" | custom-call | flops 2000000000 | bytes 1000000 | tf_op jit(solution)/shard_map/input_grad/pallas_call | solution.py:311
  129.1 0.2 collective-permute-done.5
  129.3 1.1 broadcast_select_fusion
  (17 shorter events, 0.3 us)
Async XLA Ops:
  0.6 0.9 copy-start
  1.6 10.7 %copy-start.1 = (f32[8,32,128]{2,1,0:T(8,128)S(1)}, f32[8,32,128]{2,1,0:T(8,128)}, u32[]{:S(2)}) copy-start(f32[8,32,128]{2,1,0:T(8,128)} %cot.3) | copy-start | bytes 393220
  1.6 6.7 %collective-permute-start = (f32[6,32,128]{2,1,0:T(8,128)S(1)}, f32[6,32,128]{2,1,0:T(8,128)S(1)}, u32[]{:S(2)}, u32[]{:S(2)}) collective-permute-start(f32[6,32,128]{2,1,0:T(8,128)S(1)} %pad_maximum_fusion), channel_id=1, source_target_pairs={{0,8},{8,16},{16,24},{24,32},{32,40},{40,48},{48,56},{56,64},{64,7... | collective-permute-start | bytes 294920 | tf_op jit(solution)/shard_map/ppermute | solution.py:28
  6.3 5.9 %collective-permute-start.1 = (f32[6,32,128]{2,1,0:T(8,128)S(1)}, f32[6,32,128]{2,1,0:T(8,128)S(1)}, u32[]{:S(2)}, u32[]{:S(2)}) collective-permute-start(f32[6,32,128]{2,1,0:T(8,128)S(1)} %pad_maximum_fusion.1), channel_id=1, source_target_pairs={{8,0},{16,8},{24,16},{32,24},{40,32},{48,40},{56,48},{64,56},{72,6... | collective-permute-start | bytes 294920 | tf_op jit(solution)/shard_map/ppermute | solution.py:28
  12.3 5.4 %collective-permute-start.2 = (f32[88,128]{1,0:T(8,128)S(1)}, f32[88,128]{1,0:T(8,128)S(1)}, u32[]{:S(2)}, u32[]{:S(2)}) collective-permute-start(f32[88,128]{1,0:T(8,128)S(1)} %get-tuple-element.8), channel_id=1, source_target_pairs={{0,1},{1,2},{2,3},{3,4},{4,5},{5,6},{6,7},{8,9},{9,10},{10,11},{11... | collective-permute-start | bytes 135176 | tf_op jit(solution)/shard_map/ppermute | solution.py:28
  15.5 4.8 %collective-permute-start.3 = (f32[88,128]{1,0:T(8,128)S(1)}, f32[88,128]{1,0:T(8,128)S(1)}, u32[]{:S(2)}, u32[]{:S(2)}) collective-permute-start(f32[88,128]{1,0:T(8,128)S(1)} %get-tuple-element.9), channel_id=1, source_target_pairs={{1,0},{2,1},{3,2},{4,3},{5,4},{6,5},{7,6},{9,8},{10,9},{11,10},{12... | collective-permute-start | bytes 135176 | tf_op jit(solution)/shard_map/ppermute | solution.py:28
  20.3 1.1 copy-start.2
  21.4 1.1 copy-start.3
  27.9 3.9 %collective-permute-start.4 = (f32[1152,128]{1,0:T(8,128)S(1)}, f32[1152,128]{1,0:T(8,128)S(1)}, u32[]{:S(2)}, u32[]{:S(2)}) collective-permute-start(f32[1152,128]{1,0:T(8,128)S(1)} %get-tuple-element.12), channel_id=1, source_target_pairs={{0,8},{8,0},{1,9},{9,1},{2,10},{10,2},{3,11},{11,3},{4,12},{12,4},... | collective-permute-start | bytes 1769480 | tf_op jit(solution)/shard_map/cores/ppermute | solution.py:245
  121.6 6.2 %copy-start.4 = (f32[3,3,128,128]{3,2,1,0:T(8,128)S(1)}, f32[3,3,128,128]{3,2,1,0:T(8,128)}, u32[]{:S(2)}) copy-start(f32[3,3,128,128]{3,2,1,0:T(8,128)} %filter_first.3) | copy-start | bytes 1769476
  121.6 7.7 %collective-permute-start.5 = (f32[1152,128]{1,0:T(8,128)S(1)}, f32[1152,128]{1,0:T(8,128)S(1)}, u32[]{:S(2)}, u32[]{:S(2)}) collective-permute-start(f32[1152,128]{1,0:T(8,128)S(1)} %reshape.21), channel_id=1, source_target_pairs={{0,8},{8,0},{1,9},{9,1},{2,10},{10,2},{3,11},{11,3},{4,12},{12,4},... | collective-permute-start | bytes 1769480 | tf_op jit(solution)/shard_map/cores_back/ppermute | solution.py:255

commit v4 on v3

--- a/solution.py
+++ b/solution.py
@@ -8,13 +8,13 @@
 from jax.experimental.pallas import tpu as pltpu
 from jax.sharding import Mesh, PartitionSpec as P
 
-ROWS = ("x", "z", "core")
+ROWS = ("x", "zh", "zl", "core")
 FIELD_HALO = 4
 COT_HALO = 2
 PITCH = 48
 LEFT = 8
 SLACK = 8
-VMEM_LIMIT = 40 * 2**20
+VMEM_LIMIT = 24 * 2**20
 PARAMS = pltpu.CompilerParams(vmem_limit_bytes=VMEM_LIMIT)
 IN_VMEM = pl.BlockSpec(memory_space=pltpu.VMEM)
 IN_SMEM = pl.BlockSpec(memory_space=pltpu.SMEM)
@@ -60,18 +60,16 @@
     return high, low
 
 
-def load_filter(source, flip, both, first):
-    for a in range(3):
-        if flip:
+def filters_kernel(filter_first, filter_second, forward, back):
+    for layer, source in enumerate((filter_first, filter_second)):
+        for a in range(3):
+            taps = source[a].reshape(-1, source.shape[3])
+            forward[layer, a] = jnp.concatenate(split(taps), axis=1)
             taps = jnp.concatenate([source[2 - a, 2 - b] for b in range(3)], axis=1)
-        else:
-            taps = source[a].reshape(-1, source.shape[3])
-        high, low = split(taps)
-        both[a] = jnp.concatenate([high, low], axis=0 if flip else 1)
-        first[a] = high
-
-
-def convolve(source, rows, flip, both, first, high, low):
+            back[layer, a] = jnp.concatenate(split(taps), axis=0)
+
+
+def convolve(source, rows, flip, both, high, low):
     taken = (rows + 2) * PITCH
     made = rows * PITCH
     shifts = [source[SLACK - 1 + b : SLACK - 1 + b + taken, :] for b in range(3)]
@@ -88,7 +86,10 @@
             high[start : start + made, :], both[a], dims, preferred_element_type=jnp.float32
         )
         q = lax.dot_general(
-            low[start : start + made, :], first[a], dims, preferred_element_type=jnp.float32
+            low[start : start + made, :],
+            both[a, :128] if flip else both[a, :, :128],
+            dims,
+            preferred_element_type=jnp.float32,
         )
         wide = p if wide is None else wide + p
         thin = q if thin is None else thin + q
@@ -141,10 +142,10 @@
 
 
 def main_kernel(
-    height, width, place, field, cot, low, high, from_low, from_high, filter_first, filter_second,
+    height, width, place, field, cot, low, high, from_low, from_high, forward, backward,
     kept, sent, first_delta_out,
     field_image, cot_image, hidden_image, slope_image, delta_image,
-    both, first, both_back, first_back, part_high, part_low,
+    part_high, part_low,
 ):
     a, b = FIELD_HALO, COT_HALO
     tile_rows, tile_cols, _ = field.shape
@@ -171,8 +172,7 @@
     core = place[2]
 
     rows = tile_rows + 6
-    load_filter(filter_first, False, both.at[0], first.at[0])
-    pre = convolve(field_image, rows, False, both.at[0], first.at[0], part_high, part_low)
+    pre = convolve(field_image, rows, False, forward.at[0], part_high, part_low)
     sigmoid = jax.nn.sigmoid(pre)
     slope_image[SLACK : SLACK + rows * PITCH, :] = sigmoid * (1.0 + pre * (1.0 - sigmoid))
     hidden_image[SLACK : SLACK + rows * PITCH, :] = jnp.where(
@@ -180,8 +180,7 @@
     )
 
     rows = tile_rows + 4
-    load_filter(filter_second, False, both.at[1], first.at[1])
-    pre = convolve(hidden_image, rows, False, both.at[1], first.at[1], part_high, part_low)
+    pre = convolve(hidden_image, rows, False, forward.at[1], part_high, part_low)
     sigmoid = jax.nn.sigmoid(pre)
     delta_image[SLACK : SLACK + rows * PITCH, :] = cot_image[SLACK : SLACK + rows * PITCH, :] * (
         sigmoid * (1.0 + pre * (1.0 - sigmoid))
@@ -197,8 +196,7 @@
         sent[...] = grad
 
     rows = tile_rows + 2
-    load_filter(filter_second, True, both_back, first_back)
-    back = convolve(delta_image, rows, True, both_back, first_back, part_high, part_low)
+    back = convolve(delta_image, rows, True, backward.at[1], part_high, part_low)
     start = spot(2, 0)
     first_delta_out[SLACK : SLACK + rows * PITCH, :] = jnp.where(
         inside(place, rows, 1, *grid), back * slope_image[start : start + rows * PITCH, :], 0.0
@@ -214,19 +212,12 @@
         kept[...] = grad
 
 
-def input_kernel(first_delta, filter_first, input_grad, both_back, first_back, part_high, part_low):
+def input_kernel(first_delta, backward, input_grad, part_high, part_low):
     tile_rows, tile_cols, _ = input_grad.shape
-    load_filter(filter_first, True, both_back, first_back)
-    out = convolve(first_delta, tile_rows, True, both_back, first_back, part_high, part_low)
+    out = convolve(first_delta, tile_rows, True, backward.at[0], part_high, part_low)
     for row in range(tile_rows):
         start = row * PITCH + LEFT
         input_grad[row] = out[start : start + tile_cols]
-
-
-def filters_scratch(flip):
-    if flip:
-        return [pltpu.VMEM((3, 256, 384), jnp.bfloat16), pltpu.VMEM((3, 128, 384), jnp.bfloat16)]
-    return [pltpu.VMEM((2, 3, 384, 256), jnp.bfloat16), pltpu.VMEM((2, 3, 384, 128), jnp.bfloat16)]
 
 
 def parts_scratch(rows):
@@ -248,7 +239,8 @@
         n = lax.axis_size(("x", "y"))
         mine = lax.all_to_all(mine.reshape(n, -1, channels), ("x", "y"), 0, 0).sum(0)
     with jax.named_scope("z_total"):
-        mine = to_all(mine, "z").sum(0)
+        mine = to_all(mine, "zl").sum(0)
+        mine = to_all(mine, "zh").sum(0)
     with jax.named_scope("xy_gather"):
         mine = to_all(mine, ("x", "y")).reshape(-1, channels)
     with jax.named_scope("cores_back"):
@@ -272,6 +264,18 @@
         ),
         ROWS,
     )
+    forward, backward = pl.pallas_call(
+        filters_kernel,
+        out_shape=(
+            jax.ShapeDtypeStruct((2, 3, 3 * channels, 2 * channels), jnp.bfloat16),
+            jax.ShapeDtypeStruct((2, 3, 2 * channels, 3 * channels), jnp.bfloat16),
+        ),
+        in_specs=[IN_VMEM] * 2,
+        out_specs=(IN_VMEM, IN_VMEM),
+        compiler_params=PARAMS,
+        cost_estimate=pl.CostEstimate(flops=2 * 10**9, bytes_accessed=10**6, transcendentals=0),
+        name="filters",
+    )(filter_first, filter_second)
     lines = (tile_rows + 2 * a) * a + (tile_rows + 2 * b) * b
     side = jax.ShapeDtypeStruct((lines, channels), jnp.float32)
     to_low, to_high = pl.pallas_call(
@@ -300,30 +304,28 @@
             image(tile_rows + 6),
             image(tile_rows + 6),
             image(tile_rows + 4),
-            *filters_scratch(False),
-            *filters_scratch(True),
             *parts_scratch(tile_rows + 2 * a),
         ],
         compiler_params=PARAMS,
         name="gradients",
-    )(place, field, cotangent, low, high, from_low, from_high, filter_first, filter_second)
+    )(place, field, cotangent, low, high, from_low, from_high, forward, backward)
     first_grad, second_grad = total(kept, sent)
     input_grad = pl.pallas_call(
         input_kernel,
         out_shape=jax.ShapeDtypeStruct(field.shape, jnp.float32),
         in_specs=[IN_VMEM] * 2,
         out_specs=IN_VMEM,
-        scratch_shapes=[*filters_scratch(True), *parts_scratch(delta_rows)],
+        scratch_shapes=parts_scratch(delta_rows),
         compiler_params=PARAMS,
         cost_estimate=pl.CostEstimate(flops=2 * 10**9, bytes_accessed=10**6, transcendentals=0),
         name="input_grad",
-    )(first_delta, filter_first)
+    )(first_delta, backward)
     shape = filter_first.shape
     return (input_grad, first_grad.reshape(shape), second_grad.reshape(shape))
 
 
 def solution(mesh):
-    fine = Mesh(mesh.devices.reshape(4, 16, 2, 8), ("x", "z", "core", "y"))
+    fine = Mesh(mesh.devices.reshape(4, 4, 4, 2, 8), ("x", "zh", "zl", "core", "y"))
     tile = P(ROWS, "y", None)
     return jax.shard_map(
         local, mesh=fine, in_specs=(tile, P(), P(), tile), out_specs=(tile, P(), P()), check_vma=False

time: 131 us -> 131 us (level)
  the two profiles are of different devices: /device:TPU:73 before, /device:TPU:1 now
where the time goes in v4:
time: 131 us; the launch traced here: 130 us
  blocking collectives  79.8 us (61%)
  starting transfers between devices  31.1 us (24%)
  Pallas kernels  7.02 us (5%)
  waiting for transfers between devices  5.73 us (4%)
  local copies, waits for them, and re-layouts  4.58 us (3%)
  other arithmetic  1.32 us (1%)
    all_to_all x3, blocking collectives, to_all(): return lax.all_to_all(copies, axis, 0, 0)  47 us
    all_to_all x1, blocking collectives, total(): lax.all_to_all(mine.reshape(n, -1, channels), ('x', 'y'), 0, 0).sum(0)  32.7 us
    ppermute x2, starting transfers between devices, neighbours(): lax.ppermute(high, axis, backward)  13.3 us
    ppermute x1, starting transfers between devices, total(): theirs = lax.ppermute(mine, 'core', other)  8.95 us
    ppermute x2, starting transfers between devices, neighbours(): lax.ppermute(low, axis, forward)  6.68 us
    pallas_call x1, Pallas kernels, local(): pl.pallas_call(functools.partial(main_kernel, height, width), out_shape=(...  5.32 us
    ppermute x2, waiting for transfers between devices, neighbours(): lax.ppermute(high, axis, backward)  3.87 us
    unnamed x8, local copies, waits for them, and re-layouts  2.77 us
  transfers between devices with their start and end apart: 6, of which 3 were waited for; matrix products, arithmetic and copies ran while one was open for 0% of the time, Pallas kernels for 1%

profile of v4, /device:TPU:1, one launch (start us, length us, event | category | flops | bytes accessed | tf_op | source)
XLA Modules:
  0.0 130.4 jit_solution(16110667049032679580)
XLA Ops:
  0.6 0.8 fusion.1
  1.4 0.9 fusion
  2.3 5.4 %collective-permute-start = (f32[6,32,128]{2,1,0:T(8,128)S(1)}, f32[6,32,128]{2,1,0:T(8,128)S(1)}, u32[]{:S(2)}, u32[]{:S(2)}) collective-permute-start(f32[6,32,128]{2,1,0:T(8,128)S(1)} %pad_maximum_fusion), channel_id=1, source_target_pairs={{0,8},{8,16},{16,24},{24,32},{32,40},{40,48},{48,56},{56,64},{64,7... | collective-permute-start | bytes 294920 | tf_op jit(solution)/shard_map/ppermute | solution.py:28
  7.7 12.0 %collective-permute-start.1 = (f32[6,32,128]{2,1,0:T(8,128)S(1)}, f32[6,32,128]{2,1,0:T(8,128)S(1)}, u32[]{:S(2)}, u32[]{:S(2)}) collective-permute-start(f32[6,32,128]{2,1,0:T(8,128)S(1)} %pad_maximum_fusion.1), channel_id=1, source_target_pairs={{8,0},{16,8},{24,16},{32,24},{40,32},{48,40},{56,48},{64,56},{72,6... | collective-permute-start | bytes 294920 | tf_op jit(solution)/shard_map/ppermute | solution.py:28
  19.7 1.1 copy-done.2
  20.8 1.1 copy-done.3
  21.9 0.3 filters.1
  22.2 0.6 copy-done
  22.8 0.1 copy-done.1
  22.8 1.3 collective-permute-start.2
  24.1 1.3 collective-permute-start.3
  25.4 0.1 pad_add_fusion.place
  25.5 3.9 %collective-permute-done.3.from_high = f32[88,128]{1,0:T(8,128)S(1)} collective-permute-done((f32[88,128]{1,0:T(8,128)S(1)}, f32[88,128]{1,0:T(8,128)S(1)}, u32[]{:S(2)}, u32[]{:S(2)}) %collective-permute-start.3) | collective-permute-done | bytes 45088 | tf_op jit(solution)/shard_map/ppermute | solution.py:28
  29.4 5.3 %gradients.1 = (f32[1152,128]{1,0:T(8,128)S(1)}, f32[1152,128]{1,0:T(8,128)S(1)}, f32[496,128]{1,0:T(8,128)S(1)}) custom-call(s32[3]{0:T(128)S(1)} %pad_add_fusion.place, f32[8,32,128]{2,1,0:T(8,128)S(1)} %copy-done, f32[8,32,128]{2,1,0:T(8,128)S(1)} %copy-done.1, f32[6,32,128]{2,1,0:T(8,128)S(1)} %collective-permute-done.low, ...), custom_call_target="tpu_custom_call" | custom-call | tf_op jit(solution)/shard_map/gradients/pallas_call | solution.py:292
  34.7 2.3 %collective-permute-start.4 = (f32[1152,128]{1,0:T(8,128)S(1)}, f32[1152,128]{1,0:T(8,128)S(1)}, u32[]{:S(2)}, u32[]{:S(2)}) collective-permute-start(f32[1152,128]{1,0:T(8,128)S(1)} %get-tuple-element.16), channel_id=1, source_target_pairs={{0,8},{8,0},{1,9},{9,1},{2,10},{10,2},{3,11},{11,3},{4,12},{12,4},... | collective-permute-start | bytes 1769480 | tf_op jit(solution)/shard_map/cores/ppermute | solution.py:236
  37.0 1.6 %collective-permute-done.4 = f32[1152,128]{1,0:T(8,128)S(1)} collective-permute-done((f32[1152,128]{1,0:T(8,128)S(1)}, f32[1152,128]{1,0:T(8,128)S(1)}, u32[]{:S(2)}, u32[]{:S(2)}) %collective-permute-start.4) | collective-permute-done | bytes 589856 | tf_op jit(solution)/shard_map/cores/ppermute | solution.py:236
  38.7 32.7 %all_to_all.20 = f32[32,36,128]{2,1,0:T(8,128)S(1)} all-to-all(f32[32,36,128]{2,1,0:T(8,128)S(1)} %reshape.21), channel_id=1, replica_groups=mesh['x'=4,'zh'=4,'zl'=4,'core'=2,'y'=8] {'x','y'}, dimensions={0} | all-to-all | bytes 1179648 | tf_op jit(solution)/shard_map/xy_scatter/all_to_all | solution.py:240
  71.5 7.0 %all_to_all.21 = f32[4,36,128]{2,1,0:T(8,128)S(1)} all-to-all(f32[4,36,128]{2,1,0:T(8,128)S(1)} %broadcast_in_dim.6), channel_id=1, replica_groups=mesh['x'=4,'zh'=4,'zl'=4,'core'=2,'y'=8] {'zl'}, dimensions={0} | all-to-all | bytes 147456 | tf_op jit(solution)/shard_map/z_total/all_to_all | solution.py:229
  78.6 18.0 %all_to_all.22 = f32[4,36,128]{2,1,0:T(8,128)S(1)} all-to-all(f32[4,36,128]{2,1,0:T(8,128)S(1)} %broadcast_in_dim.7), channel_id=1, replica_groups=mesh['x'=4,'zh'=4,'zl'=4,'core'=2,'y'=8] {'zh'}, dimensions={0} | all-to-all | bytes 147456 | tf_op jit(solution)/shard_map/z_total/all_to_all | solution.py:229
  96.7 22.0 %all_to_all.23 = f32[32,36,128]{2,1,0:T(8,128)S(1)} all-to-all(f32[32,36,128]{2,1,0:T(8,128)S(1)} %broadcast_in_dim.8), channel_id=1, replica_groups=mesh['x'=4,'zh'=4,'zl'=4,'core'=2,'y'=8] {'x','y'}, dimensions={0} | all-to-all | bytes 1179648 | tf_op jit(solution)/shard_map/xy_gather/all_to_all | solution.py:229
  118.7 8.9 %collective-permute-start.5 = (f32[1152,128]{1,0:T(8,128)S(1)}, f32[1152,128]{1,0:T(8,128)S(1)}, u32[]{:S(2)}, u32[]{:S(2)}) collective-permute-start(f32[1152,128]{1,0:T(8,128)S(1)} %reshape.22), channel_id=1, source_target_pairs={{0,8},{8,0},{1,9},{9,1},{2,10},{10,2},{3,11},{11,3},{4,12},{12,4},... | collective-permute-start | bytes 1769480 | tf_op jit(solution)/shard_map/cores_back/ppermute | solution.py:247
  127.7 1.4 %input_grad.1 = f32[8,32,128]{2,1,0:T(8,128)} custom-call(f32[496,128]{1,0:T(8,128)S(1)} %get-tuple-element.14.first_delta, bf16[2,3,256,384]{3,2,1,0:T(8,128)(2,1)S(1)} %get-tuple-element.13.backward), custom_call_target="tpu_custom_call" | custom-call | flops 2000000000 | bytes 1000000 | tf_op jit(solution)/shard_map/input_grad/pallas_call | solution.py:313
  129.1 0.2 collective-permute-done.5
  129.3 1.1 broadcast_select_fusion
  (19 shorter events, 0.3 us)
Async XLA Ops:
  2.3 19.8 %collective-permute-start = (f32[6,32,128]{2,1,0:T(8,128)S(1)}, f32[6,32,128]{2,1,0:T(8,128)S(1)}, u32[]{:S(2)}, u32[]{:S(2)}) collective-permute-start(f32[6,32,128]{2,1,0:T(8,128)S(1)} %pad_maximum_fusion), channel_id=1, source_target_pairs={{0,8},{8,16},{16,24},{24,32},{32,40},{40,48},{48,56},{56,64},{64,7... | collective-permute-start | bytes 294920 | tf_op jit(solution)/shard_map/ppermute | solution.py:28
  7.7 14.4 %collective-permute-start.1 = (f32[6,32,128]{2,1,0:T(8,128)S(1)}, f32[6,32,128]{2,1,0:T(8,128)S(1)}, u32[]{:S(2)}, u32[]{:S(2)}) collective-permute-start(f32[6,32,128]{2,1,0:T(8,128)S(1)} %pad_maximum_fusion.1), channel_id=1, source_target_pairs={{8,0},{16,8},{24,16},{32,24},{40,32},{48,40},{56,48},{64,56},{72,6... | collective-permute-start | bytes 294920 | tf_op jit(solution)/shard_map/ppermute | solution.py:28
  19.7 1.1 copy-start.2
  20.8 1.1 copy-start.3
  21.8 0.9 copy-start
  21.9 1.0 copy-start.1
  22.8 2.7 %collective-permute-start.2 = (f32[88,128]{1,0:T(8,128)S(1)}, f32[88,128]{1,0:T(8,128)S(1)}, u32[]{:S(2)}, u32[]{:S(2)}) collective-permute-start(f32[88,128]{1,0:T(8,128)S(1)} %get-tuple-element.10), channel_id=1, source_target_pairs={{0,1},{1,2},{2,3},{3,4},{4,5},{5,6},{6,7},{8,9},{9,10},{10,11},{11... | collective-permute-start | bytes 135176 | tf_op jit(solution)/shard_map/ppermute | solution.py:28
  24.1 5.3 %collective-permute-start.3 = (f32[88,128]{1,0:T(8,128)S(1)}, f32[88,128]{1,0:T(8,128)S(1)}, u32[]{:S(2)}, u32[]{:S(2)}) collective-permute-start(f32[88,128]{1,0:T(8,128)S(1)} %get-tuple-element.11), channel_id=1, source_target_pairs={{1,0},{2,1},{3,2},{4,3},{5,4},{6,5},{7,6},{9,8},{10,9},{11,10},{12... | collective-permute-start | bytes 135176 | tf_op jit(solution)/shard_map/ppermute | solution.py:28
  34.7 3.9 %collective-permute-start.4 = (f32[1152,128]{1,0:T(8,128)S(1)}, f32[1152,128]{1,0:T(8,128)S(1)}, u32[]{:S(2)}, u32[]{:S(2)}) collective-permute-start(f32[1152,128]{1,0:T(8,128)S(1)} %get-tuple-element.16), channel_id=1, source_target_pairs={{0,8},{8,0},{1,9},{9,1},{2,10},{10,2},{3,11},{11,3},{4,12},{12,4},... | collective-permute-start | bytes 1769480 | tf_op jit(solution)/shard_map/cores/ppermute | solution.py:236
  118.7 10.6 %collective-permute-start.5 = (f32[1152,128]{1,0:T(8,128)S(1)}, f32[1152,128]{1,0:T(8,128)S(1)}, u32[]{:S(2)}, u32[]{:S(2)}) collective-permute-start(f32[1152,128]{1,0:T(8,128)S(1)} %reshape.22), channel_id=1, source_target_pairs={{0,8},{8,0},{1,9},{9,1},{2,10},{10,2},{3,11},{11,3},{4,12},{12,4},... | collective-permute-start | bytes 1769480 | tf_op jit(solution)/shard_map/cores_back/ppermute | solution.py:247

commit v5 on v4

--- a/solution.py
+++ b/solution.py
@@ -3,6 +3,7 @@
 
 import jax
 import jax.numpy as jnp
+import numpy as np
 from jax import lax
 from jax.experimental import pallas as pl
 from jax.experimental.pallas import tpu as pltpu
@@ -16,7 +17,9 @@
 SLACK = 8
 VMEM_LIMIT = 24 * 2**20
 PARAMS = pltpu.CompilerParams(vmem_limit_bytes=VMEM_LIMIT)
+WHOLE = pltpu.CompilerParams(vmem_limit_bytes=58 * 2**20)
 IN_VMEM = pl.BlockSpec(memory_space=pltpu.VMEM)
+IN_HBM = pl.BlockSpec(memory_space=pltpu.HBM)
 IN_SMEM = pl.BlockSpec(memory_space=pltpu.SMEM)
 
 
@@ -26,6 +29,55 @@
     backward = [(target, source) for source, target in forward]
     low, high = values
     return lax.ppermute(low, axis, forward), lax.ppermute(high, axis, backward)
+
+
+def together(pairs, sems):
+    copies = [
+        pltpu.make_async_copy(source, target, sems.at[i]) for i, (source, target) in enumerate(pairs)
+    ]
+    for copy in copies:
+        copy.start()
+    return copies
+
+
+def edges_kernel(field, cot, own_field, own_cot, down, up, sems):
+    a, b = FIELD_HALO, COT_HALO
+    rows = field.shape[0]
+    copies = together(
+        (
+            (field.at[rows - a : rows], down.at[0:a]),
+            (cot.at[rows - b : rows], down.at[a : a + b]),
+            (field.at[0:a], up.at[0:a]),
+            (cot.at[0:b], up.at[a : a + b]),
+            (field, own_field),
+            (cot, own_cot),
+        ),
+        sems,
+    )
+    for copy in copies:
+        copy.wait()
+
+
+def results_kernel(place, mine, theirs, first, second, sems):
+    parts = 3
+    size = mine.shape[0] // parts
+
+    def put(first_source, second_source):
+        pairs = []
+        for part in range(parts):
+            span = slice(part * size, part * size + size)
+            pairs.append((first_source.at[span], first.at[span]))
+            pairs.append((second_source.at[span], second.at[span]))
+        for copy in together(pairs, sems):
+            copy.wait()
+
+    @pl.when(place[2] == 0)
+    def _():
+        put(theirs, mine)
+
+    @pl.when(place[2] != 0)
+    def _():
+        put(mine, theirs)
 
 
 def image(rows, dtype=jnp.float32):
@@ -60,8 +112,16 @@
     return high, low
 
 
-def filters_kernel(filter_first, filter_second, forward, back):
-    for layer, source in enumerate((filter_first, filter_second)):
+def filters_kernel(filter_first, filter_second, forward, back, held, sems):
+    sources = (filter_first, filter_second)
+    copies = together(
+        [(source.at[a], held.at[layer, a]) for layer, source in enumerate(sources) for a in range(3)],
+        sems,
+    )
+    for layer in range(2):
+        source = held.at[layer]
+        for a in range(3):
+            copies[3 * layer + a].wait()
         for a in range(3):
             taps = source[a].reshape(-1, source.shape[3])
             forward[layer, a] = jnp.concatenate(split(taps), axis=1)
@@ -224,30 +284,48 @@
     return [pltpu.VMEM((rows * PITCH, 384), jnp.bfloat16)] * 2
 
 
-def to_all(values, axis):
-    copies = jnp.broadcast_to(values[None], (lax.axis_size(axis),) + values.shape)
-    return lax.all_to_all(copies, axis, 0, 0)
+ALL = ("x", "zh", "zl", "core", "y")
+
+
+def groups(kinds):
+    sizes = [lax.axis_size(axis) for axis in ALL[:4]] + [lax.axis_size("y") // 2, 2]
+    names = ["x", "zh", "zl", "core", "yh", "yl"]
+    ids = np.arange(math.prod(sizes)).reshape(sizes)
+    found = []
+    for core, inner in enumerate(kinds):
+        outer = [name for name in names if name not in inner]
+        order = [names.index(name) for name in outer + list(inner)]
+        moved = np.take(ids, [core], axis=3).transpose(order)
+        found.append(moved.reshape(-1, math.prod(sizes[names.index(name)] for name in inner)))
+    return np.concatenate(found).tolist()
+
+
+def exchange(parts, kinds):
+    return lax.all_to_all(parts, ALL, 0, 0, axis_index_groups=groups(kinds))
+
+
+def to_all(values, kinds):
+    count = len(groups(kinds)[0])
+    return exchange(jnp.broadcast_to(values[None], (count,) + values.shape), kinds)
 
 
 def total(mine, theirs):
-    core = lax.axis_index("core")
     other = [(0, 1), (1, 0)]
+    plane = (("x", "yh", "yl"), ("x", "zl", "yl"))
     with jax.named_scope("cores"):
         mine = mine + lax.ppermute(theirs, "core", other)
     channels = mine.shape[-1]
-    with jax.named_scope("xy_scatter"):
-        n = lax.axis_size(("x", "y"))
-        mine = lax.all_to_all(mine.reshape(n, -1, channels), ("x", "y"), 0, 0).sum(0)
-    with jax.named_scope("z_total"):
-        mine = to_all(mine, "zl").sum(0)
-        mine = to_all(mine, "zh").sum(0)
-    with jax.named_scope("xy_gather"):
-        mine = to_all(mine, ("x", "y")).reshape(-1, channels)
+    with jax.named_scope("plane_scatter"):
+        n = len(groups(plane)[0])
+        mine = exchange(mine.reshape(n, -1, channels), plane).sum(0)
+    with jax.named_scope("rest_total"):
+        mine = to_all(mine, (("zl",), ("yh",))).sum(0)
+        mine = to_all(mine, (("zh",), ("zh",))).sum(0)
+    with jax.named_scope("plane_gather"):
+        mine = to_all(mine, plane).reshape(-1, channels)
     with jax.named_scope("cores_back"):
         theirs = lax.ppermute(mine, "core", other)
-    first = jnp.where(core == 0, theirs, mine)
-    second = jnp.where(core == 0, mine, theirs)
-    return first, second
+    return mine, theirs
 
 
 def local(field, filter_first, filter_second, cotangent):
@@ -257,22 +335,31 @@
     width = tile_cols * lax.axis_size("y")
     place = jnp.stack([lax.axis_index(ROWS), lax.axis_index("y"), lax.axis_index("core")])
     place = place.astype(jnp.int32)
-    low, high = neighbours(
-        (
-            jnp.concatenate([field[-a:], cotangent[-b:]], axis=0),
-            jnp.concatenate([field[:a], cotangent[:b]], axis=0),
-        ),
-        ROWS,
-    )
+    edge = jax.ShapeDtypeStruct((a + b, tile_cols, channels), jnp.float32)
+    tile = jax.ShapeDtypeStruct(field.shape, jnp.float32)
+    field, cotangent, down, up = pl.pallas_call(
+        edges_kernel,
+        out_shape=(tile, tile, edge, edge),
+        in_specs=[IN_HBM] * 2,
+        out_specs=(IN_VMEM,) * 4,
+        scratch_shapes=[pltpu.SemaphoreType.DMA((6,))],
+        compiler_params=WHOLE,
+        name="edges",
+    )(field, cotangent)
+    low, high = neighbours((down, up), ROWS)
     forward, backward = pl.pallas_call(
         filters_kernel,
         out_shape=(
             jax.ShapeDtypeStruct((2, 3, 3 * channels, 2 * channels), jnp.bfloat16),
             jax.ShapeDtypeStruct((2, 3, 2 * channels, 3 * channels), jnp.bfloat16),
         ),
-        in_specs=[IN_VMEM] * 2,
+        in_specs=[IN_HBM] * 2,
         out_specs=(IN_VMEM, IN_VMEM),
-        compiler_params=PARAMS,
+        scratch_shapes=[
+            pltpu.VMEM((2,) + filter_first.shape, jnp.float32),
+            pltpu.SemaphoreType.DMA((6,)),
+        ],
+        compiler_params=WHOLE,
         cost_estimate=pl.CostEstimate(flops=2 * 10**9, bytes_accessed=10**6, transcendentals=0),
         name="filters",
     )(filter_first, filter_second)
@@ -309,7 +396,7 @@
         compiler_params=PARAMS,
         name="gradients",
     )(place, field, cotangent, low, high, from_low, from_high, forward, backward)
-    first_grad, second_grad = total(kept, sent)
+    mine, theirs = total(kept, sent)
     input_grad = pl.pallas_call(
         input_kernel,
         out_shape=jax.ShapeDtypeStruct(field.shape, jnp.float32),
@@ -320,6 +407,15 @@
         cost_estimate=pl.CostEstimate(flops=2 * 10**9, bytes_accessed=10**6, transcendentals=0),
         name="input_grad",
     )(first_delta, backward)
+    first_grad, second_grad = pl.pallas_call(
+        results_kernel,
+        out_shape=(grad, grad),
+        in_specs=[IN_SMEM, IN_VMEM, IN_VMEM],
+        out_specs=(IN_HBM, IN_HBM),
+        scratch_shapes=[pltpu.SemaphoreType.DMA((6,))],
+        compiler_params=PARAMS,
+        name="results",
+    )(place, mine, theirs)
     shape = filter_first.shape
     return (input_grad, first_grad.reshape(shape), second_grad.reshape(shape))
 

time: 131 us -> 129 us (0.985)
  Pallas kernels: 7.02 us -> 13.2 us
  blocking collectives: 79.8 us -> 75.3 us
  local copies, waits for them, and re-layouts: 4.58 us -> 2.7 us
    all_to_all x4, blocking collectives: 79.8 us -> 75.3 us  [exchange(): return lax.all_to_all(parts, ALL, 0, 0, axis_index_groups=groups(kinds))]
    pallas_call x0 -> x2, Pallas kernels: none -> 3.49 us  [the longest x1 1.88 us: local(): pl.pallas_call(edges_kernel, out_shape=(tile, tile, edge, edge), in_specs...]
    pallas_call x1, Pallas kernels: 0.29 us -> 2.94 us  [local(): pl.pallas_call(filters_kernel, out_shape=(jax.ShapeDtypeStruct((2, 3, 3 *...]
    slice x2 -> x0, local copies, waits for them, and re-layouts: 1.66 us -> none  [the longest x1 0.88 us: local(): field[:a]]
    unnamed x8 -> x10, local copies, waits for them, and re-layouts: 2.77 us -> 2.56 us
  transfers between devices with their start and end apart: 6 -> 6, of which waited for: 3 -> 3; matrix products, arithmetic and copies ran while one was open for 0% -> 0% of each run, Pallas kernels for 1% -> 3%
where the time goes in v5:
time: 129 us; the launch traced here: 128 us
  blocking collectives  75.3 us (58%)
  starting transfers between devices  30.1 us (23%)
  Pallas kernels  13.2 us (10%)
  waiting for transfers between devices  5.72 us (4%)
  local copies, waits for them, and re-layouts  2.7 us (2%)
    all_to_all x4, blocking collectives, exchange(): return lax.all_to_all(parts, ALL, 0, 0, axis_index_groups=groups(kinds))  75.3 us
    ppermute x2, starting transfers between devices, neighbours(): lax.ppermute(high, axis, backward)  13.3 us
    ppermute x1, starting transfers between devices, total(): theirs = lax.ppermute(mine, 'core', other)  7.91 us
    ppermute x2, starting transfers between devices, neighbours(): lax.ppermute(low, axis, forward)  6.68 us
    pallas_call x1, Pallas kernels, local(): pl.pallas_call(functools.partial(main_kernel, height, width), out_shape=(...  5.33 us
    ppermute x2, waiting for transfers between devices, neighbours(): lax.ppermute(high, axis, backward)  3.87 us
    pallas_call x1, Pallas kernels, local(): pl.pallas_call(filters_kernel, out_shape=(jax.ShapeDtypeStruct((2, 3, 3 *...  2.94 us
  transfers between devices with their start and end apart: 6, of which 3 were waited for; matrix products, arithmetic and copies ran while one was open for 0% of the time, Pallas kernels for 3%

profile of v5, /device:TPU:1, one launch (start us, length us, event | category | flops | bytes accessed | tf_op | source)
XLA Modules:
  0.0 128.1 jit_solution(13355563765051268726)
XLA Ops:
  0.6 1.9 %edges.1 = (f32[8,32,128]{2,1,0:T(8,128)}, f32[8,32,128]{2,1,0:T(8,128)}, f32[6,32,128]{2,1,0:T(8,128)}, f32[6,32,128]{2,1,0:T(8,128)}) custom-call(f32[8,32,128]{2,1,0:T(8,128)} %field.1, f32[8,32,128]{2,1,0:T(8,128)} %cot.1), custom_call_target="tpu_custom_call" | custom-call | tf_op jit(solution)/shard_map/edges/pallas_call | solution.py:340
  2.5 5.4 %collective-permute-start = (f32[6,32,128]{2,1,0:T(8,128)}, f32[6,32,128]{2,1,0:T(8,128)S(1)}, u32[]{:S(2)}, u32[]{:S(2)}) collective-permute-start(f32[6,32,128]{2,1,0:T(8,128)} %get-tuple-element.18), channel_id=1, source_target_pairs={{0,8},{8,16},{16,24},{24,32},{32,40},{40,48},{48,56},{56,64},{64,7... | collective-permute-start | bytes 294920 | tf_op jit(solution)/shard_map/ppermute | solution.py:31
  7.9 12.0 %collective-permute-start.1 = (f32[6,32,128]{2,1,0:T(8,128)}, f32[6,32,128]{2,1,0:T(8,128)S(1)}, u32[]{:S(2)}, u32[]{:S(2)}) collective-permute-start(f32[6,32,128]{2,1,0:T(8,128)} %get-tuple-element.19), channel_id=1, source_target_pairs={{8,0},{16,8},{24,16},{32,24},{40,32},{48,40},{56,48},{64,56},{72,6... | collective-permute-start | bytes 294920 | tf_op jit(solution)/shard_map/ppermute | solution.py:31
  19.9 0.0 copy-start.3
  19.9 2.9 %filters.1 = (bf16[2,3,384,256]{3,2,1,0:T(8,128)(2,1)}, bf16[2,3,256,384]{3,2,1,0:T(8,128)(2,1)}) custom-call(f32[3,3,128,128]{3,2,1,0:T(8,128)} %filter_first.1, f32[3,3,128,128]{3,2,1,0:T(8,128)} %filter_second.1), custom_call_target="tpu_custom_call" | custom-call | flops 2000000000 | bytes 1000000 | tf_op jit(solution)/shard_map/filters/pallas_call | solution.py:350
  23.0 1.3 %collective-permute-start.2 = (f32[88,128]{1,0:T(8,128)S(1)}, f32[88,128]{1,0:T(8,128)S(1)}, u32[]{:S(2)}, u32[]{:S(2)}) collective-permute-start(f32[88,128]{1,0:T(8,128)S(1)} %get-tuple-element.20), channel_id=1, source_target_pairs={{0,1},{1,2},{2,3},{3,4},{4,5},{5,6},{6,7},{8,9},{9,10},{10,11},{11... | collective-permute-start | bytes 135176 | tf_op jit(solution)/shard_map/ppermute | solution.py:31
  24.3 1.3 %collective-permute-start.3 = (f32[88,128]{1,0:T(8,128)S(1)}, f32[88,128]{1,0:T(8,128)S(1)}, u32[]{:S(2)}, u32[]{:S(2)}) collective-permute-start(f32[88,128]{1,0:T(8,128)S(1)} %get-tuple-element.21), channel_id=1, source_target_pairs={{1,0},{2,1},{3,2},{4,3},{5,4},{6,5},{7,6},{9,8},{10,9},{11,10},{12... | collective-permute-start | bytes 135176 | tf_op jit(solution)/shard_map/ppermute | solution.py:31
  25.6 0.1 pad_add_fusion.place
  25.6 3.9 %collective-permute-done.3.from_high = f32[88,128]{1,0:T(8,128)S(1)} collective-permute-done((f32[88,128]{1,0:T(8,128)S(1)}, f32[88,128]{1,0:T(8,128)S(1)}, u32[]{:S(2)}, u32[]{:S(2)}) %collective-permute-start.3) | collective-permute-done | bytes 45088 | tf_op jit(solution)/shard_map/ppermute | solution.py:31
  29.5 1.3 copy-done
  30.8 1.3 copy-done.2
  32.1 5.3 %gradients.1 = (f32[1152,128]{1,0:T(8,128)S(1)}, f32[1152,128]{1,0:T(8,128)S(1)}, f32[496,128]{1,0:T(8,128)S(1)}) custom-call(s32[3]{0:T(128)S(1)} %pad_add_fusion.place, f32[8,32,128]{2,1,0:T(8,128)S(1)} %copy-done.3, f32[8,32,128]{2,1,0:T(8,128)S(1)} %copy-done.4, f32[6,32,128]{2,1,0:T(8,128)S(1)} %collective-permute-done.low, ...), custom_call_target="tpu_custom_call" | custom-call | tf_op jit(solution)/shard_map/gradients/pallas_call | solution.py:379
  37.4 2.3 %collective-permute-start.4 = (f32[1152,128]{1,0:T(8,128)S(1)}, f32[1152,128]{1,0:T(8,128)S(1)}, u32[]{:S(2)}, u32[]{:S(2)}) collective-permute-start(f32[1152,128]{1,0:T(8,128)S(1)} %get-tuple-element.26), channel_id=1, source_target_pairs={{0,8},{8,0},{1,9},{9,1},{2,10},{10,2},{3,11},{11,3},{4,12},{12,4},... | collective-permute-start | bytes 1769480 | tf_op jit(solution)/shard_map/cores/ppermute | solution.py:316
  39.7 1.6 %collective-permute-done.4 = f32[1152,128]{1,0:T(8,128)S(1)} collective-permute-done((f32[1152,128]{1,0:T(8,128)S(1)}, f32[1152,128]{1,0:T(8,128)S(1)}, u32[]{:S(2)}, u32[]{:S(2)}) %collective-permute-start.4) | collective-permute-done | bytes 589856 | tf_op jit(solution)/shard_map/cores/ppermute | solution.py:316
  41.3 0.1 add.15
  41.4 25.0 %all_to_all.20 = f32[32,36,128]{2,1,0:T(8,128)S(1)} all-to-all(f32[32,36,128]{2,1,0:T(8,128)S(1)} %reshape.21), channel_id=1, replica_groups={{0,1,2,3,4,5,6,7,256,257,258,259,260,261,262,263,512,513,514,515,516,51..., dimensions={0} | all-to-all | bytes 1179648 | tf_op jit(solution)/shard_map/plane_scatter/all_to_all | solution.py:304
  66.4 0.1 reduce_sum.27
  66.5 12.8 %all_to_all.21 = f32[4,36,128]{2,1,0:T(8,128)S(1)} all-to-all(f32[4,36,128]{2,1,0:T(8,128)S(1)} %broadcast_in_dim.6), channel_id=1, replica_groups={{0,16,32,48},{1,17,33,49},{2,18,34,50},{3,19,35,51},{4,20,36,52},{5,21,..., dimensions={0} | all-to-all | bytes 147456 | tf_op jit(solution)/shard_map/rest_total/all_to_all | solution.py:304
  79.3 19.3 %all_to_all.22 = f32[4,36,128]{2,1,0:T(8,128)S(1)} all-to-all(f32[4,36,128]{2,1,0:T(8,128)S(1)} %broadcast_in_dim.7), channel_id=1, replica_groups={{0,64,128,192},{1,65,129,193},{2,66,130,194},{3,67,131,195},{4,68,132,1..., dimensions={0} | all-to-all | bytes 147456 | tf_op jit(solution)/shard_map/rest_total/all_to_all | solution.py:304
  98.6 18.3 %all_to_all.23 = f32[32,36,128]{2,1,0:T(8,128)S(1)} all-to-all(f32[32,36,128]{2,1,0:T(8,128)S(1)} %broadcast_in_dim.8), channel_id=1, replica_groups={{0,1,2,3,4,5,6,7,256,257,258,259,260,261,262,263,512,513,514,515,516,51..., dimensions={0} | all-to-all | bytes 1179648 | tf_op jit(solution)/shard_map/plane_gather/all_to_all | solution.py:304
  117.0 7.9 %collective-permute-start.5 = (f32[1152,128]{1,0:T(8,128)S(1)}, f32[1152,128]{1,0:T(8,128)S(1)}, u32[]{:S(2)}, u32[]{:S(2)}) collective-permute-start(f32[1152,128]{1,0:T(8,128)S(1)} %reshape.22.mine), channel_id=1, source_target_pairs={{0,8},{8,0},{1,9},{9,1},{2,10},{10,2},{3,11},{11,3},{4,12},{12,4},... | collective-permute-start | bytes 1769480 | tf_op jit(solution)/shard_map/cores_back/ppermute | solution.py:327
  124.9 1.4 %input_grad.1 = f32[8,32,128]{2,1,0:T(8,128)} custom-call(f32[496,128]{1,0:T(8,128)S(1)} %get-tuple-element.24.first_delta, bf16[2,3,256,384]{3,2,1,0:T(8,128)(2,1)S(1)} %copy-done.1), custom_call_target="tpu_custom_call" | custom-call | flops 2000000000 | bytes 1000000 | tf_op jit(solution)/shard_map/input_grad/pallas_call | solution.py:400
  126.3 0.2 collective-permute-done.5.theirs
  126.5 1.6 %results.1 = (f32[1152,128]{1,0:T(8,128)}, f32[1152,128]{1,0:T(8,128)}) custom-call(s32[3]{0:T(128)S(1)} %pad_add_fusion.place, f32[1152,128]{1,0:T(8,128)S(1)} %reshape.22.mine, f32[1152,128]{1,0:T(8,128)S(1)} %collective-permute-done.5.theirs), custom_call_target="tpu_custom_call" | custom-call | tf_op jit(solution)/shard_map/results/pallas_call | solution.py:410
  (18 shorter events, 0.2 us)
Async XLA Ops:
  2.5 20.4 %collective-permute-start = (f32[6,32,128]{2,1,0:T(8,128)}, f32[6,32,128]{2,1,0:T(8,128)S(1)}, u32[]{:S(2)}, u32[]{:S(2)}) collective-permute-start(f32[6,32,128]{2,1,0:T(8,128)} %get-tuple-element.18), channel_id=1, source_target_pairs={{0,8},{8,16},{16,24},{24,32},{32,40},{40,48},{48,56},{56,64},{64,7... | collective-permute-start | bytes 294920 | tf_op jit(solution)/shard_map/ppermute | solution.py:31
  7.9 15.0 %collective-permute-start.1 = (f32[6,32,128]{2,1,0:T(8,128)}, f32[6,32,128]{2,1,0:T(8,128)S(1)}, u32[]{:S(2)}, u32[]{:S(2)}) collective-permute-start(f32[6,32,128]{2,1,0:T(8,128)} %get-tuple-element.19), channel_id=1, source_target_pairs={{8,0},{16,8},{24,16},{32,24},{40,32},{48,40},{56,48},{64,56},{72,6... | collective-permute-start | bytes 294920 | tf_op jit(solution)/shard_map/ppermute | solution.py:31
  19.9 3.0 %copy-start.3 = (f32[8,32,128]{2,1,0:T(8,128)S(1)}, f32[8,32,128]{2,1,0:T(8,128)}, u32[]{:S(2)}) copy-start(f32[8,32,128]{2,1,0:T(8,128)} %get-tuple-element.16.field) | copy-start | bytes 393220
  19.9 3.0 %copy-start.4 = (f32[8,32,128]{2,1,0:T(8,128)S(1)}, f32[8,32,128]{2,1,0:T(8,128)}, u32[]{:S(2)}) copy-start(f32[8,32,128]{2,1,0:T(8,128)} %get-tuple-element.17.cot) | copy-start | bytes 393220
  23.0 2.7 %collective-permute-start.2 = (f32[88,128]{1,0:T(8,128)S(1)}, f32[88,128]{1,0:T(8,128)S(1)}, u32[]{:S(2)}, u32[]{:S(2)}) collective-permute-start(f32[88,128]{1,0:T(8,128)S(1)} %get-tuple-element.20), channel_id=1, source_target_pairs={{0,1},{1,2},{2,3},{3,4},{4,5},{5,6},{6,7},{8,9},{9,10},{10,11},{11... | collective-permute-start | bytes 135176 | tf_op jit(solution)/shard_map/ppermute | solution.py:31
  24.3 5.3 %collective-permute-start.3 = (f32[88,128]{1,0:T(8,128)S(1)}, f32[88,128]{1,0:T(8,128)S(1)}, u32[]{:S(2)}, u32[]{:S(2)}) collective-permute-start(f32[88,128]{1,0:T(8,128)S(1)} %get-tuple-element.21), channel_id=1, source_target_pairs={{1,0},{2,1},{3,2},{4,3},{5,4},{6,5},{7,6},{9,8},{10,9},{11,10},{12... | collective-permute-start | bytes 135176 | tf_op jit(solution)/shard_map/ppermute | solution.py:31
  29.5 1.3 copy-start
  30.8 1.3 copy-start.2
  37.4 3.9 %collective-permute-start.4 = (f32[1152,128]{1,0:T(8,128)S(1)}, f32[1152,128]{1,0:T(8,128)S(1)}, u32[]{:S(2)}, u32[]{:S(2)}) collective-permute-start(f32[1152,128]{1,0:T(8,128)S(1)} %get-tuple-element.26), channel_id=1, source_target_pairs={{0,8},{8,0},{1,9},{9,1},{2,10},{10,2},{3,11},{11,3},{4,12},{12,4},... | collective-permute-start | bytes 1769480 | tf_op jit(solution)/shard_map/cores/ppermute | solution.py:316
  98.6 26.3 %copy-start.1 = (bf16[2,3,256,384]{3,2,1,0:T(8,128)(2,1)S(1)}, bf16[2,3,256,384]{3,2,1,0:T(8,128)(2,1)}, u32[]{:S(2)}) copy-start(bf16[2,3,256,384]{3,2,1,0:T(8,128)(2,1)} %get-tuple-element.23.backward) | copy-start | bytes 3538948
  117.0 9.5 %collective-permute-start.5 = (f32[1152,128]{1,0:T(8,128)S(1)}, f32[1152,128]{1,0:T(8,128)S(1)}, u32[]{:S(2)}, u32[]{:S(2)}) collective-permute-start(f32[1152,128]{1,0:T(8,128)S(1)} %reshape.22.mine), channel_id=1, source_target_pairs={{0,8},{8,0},{1,9},{9,1},{2,10},{10,2},{3,11},{11,3},{4,12},{12,4},... | collective-permute-start | bytes 1769480 | tf_op jit(solution)/shard_map/cores_back/ppermute | solution.py:327

commit v6 on v4

--- a/solution.py
+++ b/solution.py
@@ -3,6 +3,7 @@
 
 import jax
 import jax.numpy as jnp
+import numpy as np
 from jax import lax
 from jax.experimental import pallas as pl
 from jax.experimental.pallas import tpu as pltpu
@@ -224,30 +225,48 @@
     return [pltpu.VMEM((rows * PITCH, 384), jnp.bfloat16)] * 2
 
 
-def to_all(values, axis):
-    copies = jnp.broadcast_to(values[None], (lax.axis_size(axis),) + values.shape)
-    return lax.all_to_all(copies, axis, 0, 0)
+ALL = ("x", "zh", "zl", "core", "y")
+
+
+def groups(kinds):
+    sizes = [lax.axis_size(axis) for axis in ALL[:4]] + [lax.axis_size("y") // 2, 2]
+    names = ["x", "zh", "zl", "core", "yh", "yl"]
+    ids = np.arange(math.prod(sizes)).reshape(sizes)
+    found = []
+    for core, inner in enumerate(kinds):
+        outer = [name for name in names if name not in inner]
+        order = [names.index(name) for name in outer + list(inner)]
+        moved = np.take(ids, [core], axis=3).transpose(order)
+        found.append(moved.reshape(-1, math.prod(sizes[names.index(name)] for name in inner)))
+    return np.concatenate(found).tolist()
+
+
+def exchange(parts, kinds):
+    return lax.all_to_all(parts, ALL, 0, 0, axis_index_groups=groups(kinds))
+
+
+def to_all(values, kinds):
+    count = len(groups(kinds)[0])
+    return exchange(jnp.broadcast_to(values[None], (count,) + values.shape), kinds)
 
 
 def total(mine, theirs):
-    core = lax.axis_index("core")
     other = [(0, 1), (1, 0)]
+    plane = (("x", "yh", "yl"), ("x", "zl", "yl"))
     with jax.named_scope("cores"):
         mine = mine + lax.ppermute(theirs, "core", other)
     channels = mine.shape[-1]
-    with jax.named_scope("xy_scatter"):
-        n = lax.axis_size(("x", "y"))
-        mine = lax.all_to_all(mine.reshape(n, -1, channels), ("x", "y"), 0, 0).sum(0)
-    with jax.named_scope("z_total"):
-        mine = to_all(mine, "zl").sum(0)
-        mine = to_all(mine, "zh").sum(0)
-    with jax.named_scope("xy_gather"):
-        mine = to_all(mine, ("x", "y")).reshape(-1, channels)
+    with jax.named_scope("plane_scatter"):
+        n = len(groups(plane)[0])
+        mine = exchange(mine.reshape(n, -1, channels), plane).sum(0)
+    with jax.named_scope("rest_total"):
+        mine = to_all(mine, (("zl",), ("yh",))).sum(0)
+        mine = to_all(mine, (("zh",), ("zh",))).sum(0)
+    with jax.named_scope("plane_gather"):
+        mine = to_all(mine, plane).reshape(-1, channels)
     with jax.named_scope("cores_back"):
         theirs = lax.ppermute(mine, "core", other)
-    first = jnp.where(core == 0, theirs, mine)
-    second = jnp.where(core == 0, mine, theirs)
-    return first, second
+    return mine, theirs
 
 
 def local(field, filter_first, filter_second, cotangent):
@@ -309,7 +328,10 @@
         compiler_params=PARAMS,
         name="gradients",
     )(place, field, cotangent, low, high, from_low, from_high, forward, backward)
-    first_grad, second_grad = total(kept, sent)
+    mine, theirs = total(kept, sent)
+    holds_second = place[2] == 0
+    first_grad = jnp.where(holds_second, theirs, mine)
+    second_grad = jnp.where(holds_second, mine, theirs)
     input_grad = pl.pallas_call(
         input_kernel,
         out_shape=jax.ShapeDtypeStruct(field.shape, jnp.float32),

time: 131 us -> 126 us (0.962)
  blocking collectives: 79.8 us -> 74.9 us
    all_to_all x4, blocking collectives: 79.8 us -> 74.9 us  [exchange(): return lax.all_to_all(parts, ALL, 0, 0, axis_index_groups=groups(kinds))]
where the time goes in v6:
time: 126 us; the launch traced here: 124 us
  blocking collectives  74.9 us (59%)
  starting transfers between devices  30.1 us (24%)
  Pallas kernels  7.02 us (6%)
  waiting for transfers between devices  5.73 us (5%)
  local copies, waits for them, and re-layouts  4.58 us (4%)
  other arithmetic  1.32 us (1%)
    all_to_all x4, blocking collectives, exchange(): return lax.all_to_all(parts, ALL, 0, 0, axis_index_groups=groups(kinds))  74.9 us
    ppermute x2, starting transfers between devices, neighbours(): lax.ppermute(high, axis, backward)  13.3 us
    ppermute x1, starting transfers between devices, total(): theirs = lax.ppermute(mine, 'core', other)  7.94 us
    ppermute x2, starting transfers between devices, neighbours(): lax.ppermute(low, axis, forward)  6.68 us
    pallas_call x1, Pallas kernels, local(): pl.pallas_call(functools.partial(main_kernel, height, width), out_shape=(...  5.32 us
    ppermute x2, waiting for transfers between devices, neighbours(): lax.ppermute(high, axis, backward)  3.87 us
    unnamed x8, local copies, waits for them, and re-layouts  2.77 us
  transfers between devices with their start and end apart: 6, of which 3 were waited for; matrix products, arithmetic and copies ran while one was open for 0% of the time, Pallas kernels for 1%

profile of v6, /device:TPU:1, one launch (start us, length us, event | category | flops | bytes accessed | tf_op | source)
XLA Modules:
  0.0 124.5 jit_solution(11196804930226838560)
XLA Ops:
  0.6 0.8 fusion.1
  1.4 0.9 fusion
  2.3 5.4 %collective-permute-start = (f32[6,32,128]{2,1,0:T(8,128)S(1)}, f32[6,32,128]{2,1,0:T(8,128)S(1)}, u32[]{:S(2)}, u32[]{:S(2)}) collective-permute-start(f32[6,32,128]{2,1,0:T(8,128)S(1)} %pad_maximum_fusion), channel_id=1, source_target_pairs={{0,8},{8,16},{16,24},{24,32},{32,40},{40,48},{48,56},{56,64},{64,7... | collective-permute-start | bytes 294920 | tf_op jit(solution)/shard_map/ppermute | solution.py:29
  7.7 12.0 %collective-permute-start.1 = (f32[6,32,128]{2,1,0:T(8,128)S(1)}, f32[6,32,128]{2,1,0:T(8,128)S(1)}, u32[]{:S(2)}, u32[]{:S(2)}) collective-permute-start(f32[6,32,128]{2,1,0:T(8,128)S(1)} %pad_maximum_fusion.1), channel_id=1, source_target_pairs={{8,0},{16,8},{24,16},{32,24},{40,32},{48,40},{56,48},{64,56},{72,6... | collective-permute-start | bytes 294920 | tf_op jit(solution)/shard_map/ppermute | solution.py:29
  19.7 1.1 copy-done.2
  20.8 1.1 copy-done.3
  21.9 0.3 filters.1
  22.2 0.6 copy-done
  22.8 0.1 copy-done.1
  22.8 1.3 %collective-permute-start.2 = (f32[88,128]{1,0:T(8,128)S(1)}, f32[88,128]{1,0:T(8,128)S(1)}, u32[]{:S(2)}, u32[]{:S(2)}) collective-permute-start(f32[88,128]{1,0:T(8,128)S(1)} %get-tuple-element.10), channel_id=1, source_target_pairs={{0,1},{1,2},{2,3},{3,4},{4,5},{5,6},{6,7},{8,9},{9,10},{10,11},{11... | collective-permute-start | bytes 135176 | tf_op jit(solution)/shard_map/ppermute | solution.py:29
  24.1 1.3 %collective-permute-start.3 = (f32[88,128]{1,0:T(8,128)S(1)}, f32[88,128]{1,0:T(8,128)S(1)}, u32[]{:S(2)}, u32[]{:S(2)}) collective-permute-start(f32[88,128]{1,0:T(8,128)S(1)} %get-tuple-element.11), channel_id=1, source_target_pairs={{1,0},{2,1},{3,2},{4,3},{5,4},{6,5},{7,6},{9,8},{10,9},{11,10},{12... | collective-permute-start | bytes 135176 | tf_op jit(solution)/shard_map/ppermute | solution.py:29
  25.4 0.1 pad_add_fusion.place
  25.5 3.9 %collective-permute-done.3.from_high = f32[88,128]{1,0:T(8,128)S(1)} collective-permute-done((f32[88,128]{1,0:T(8,128)S(1)}, f32[88,128]{1,0:T(8,128)S(1)}, u32[]{:S(2)}, u32[]{:S(2)}) %collective-permute-start.3) | collective-permute-done | bytes 45088 | tf_op jit(solution)/shard_map/ppermute | solution.py:29
  29.4 5.3 %gradients.1 = (f32[1152,128]{1,0:T(8,128)S(1)}, f32[1152,128]{1,0:T(8,128)S(1)}, f32[496,128]{1,0:T(8,128)S(1)}) custom-call(s32[3]{0:T(128)S(1)} %pad_add_fusion.place, f32[8,32,128]{2,1,0:T(8,128)S(1)} %copy-done, f32[8,32,128]{2,1,0:T(8,128)S(1)} %copy-done.1, f32[6,32,128]{2,1,0:T(8,128)S(1)} %collective-permute-done.low, ...), custom_call_target="tpu_custom_call" | custom-call | tf_op jit(solution)/shard_map/gradients/pallas_call | solution.py:311
  34.7 2.3 %collective-permute-start.4 = (f32[1152,128]{1,0:T(8,128)S(1)}, f32[1152,128]{1,0:T(8,128)S(1)}, u32[]{:S(2)}, u32[]{:S(2)}) collective-permute-start(f32[1152,128]{1,0:T(8,128)S(1)} %get-tuple-element.16), channel_id=1, source_target_pairs={{0,8},{8,0},{1,9},{9,1},{2,10},{10,2},{3,11},{11,3},{4,12},{12,4},... | collective-permute-start | bytes 1769480 | tf_op jit(solution)/shard_map/cores/ppermute | solution.py:257
  37.0 1.6 %collective-permute-done.4 = f32[1152,128]{1,0:T(8,128)S(1)} collective-permute-done((f32[1152,128]{1,0:T(8,128)S(1)}, f32[1152,128]{1,0:T(8,128)S(1)}, u32[]{:S(2)}, u32[]{:S(2)}) %collective-permute-start.4) | collective-permute-done | bytes 589856 | tf_op jit(solution)/shard_map/cores/ppermute | solution.py:257
  38.7 25.0 %all_to_all.20 = f32[32,36,128]{2,1,0:T(8,128)S(1)} all-to-all(f32[32,36,128]{2,1,0:T(8,128)S(1)} %reshape.21), channel_id=1, replica_groups={{0,1,2,3,4,5,6,7,256,257,258,259,260,261,262,263,512,513,514,515,516,51..., dimensions={0} | all-to-all | bytes 1179648 | tf_op jit(solution)/shard_map/plane_scatter/all_to_all | solution.py:245
  63.8 12.8 %all_to_all.21 = f32[4,36,128]{2,1,0:T(8,128)S(1)} all-to-all(f32[4,36,128]{2,1,0:T(8,128)S(1)} %broadcast_in_dim.6), channel_id=1, replica_groups={{0,16,32,48},{1,17,33,49},{2,18,34,50},{3,19,35,51},{4,20,36,52},{5,21,..., dimensions={0} | all-to-all | bytes 147456 | tf_op jit(solution)/shard_map/rest_total/all_to_all | solution.py:245
  76.6 19.0 %all_to_all.22 = f32[4,36,128]{2,1,0:T(8,128)S(1)} all-to-all(f32[4,36,128]{2,1,0:T(8,128)S(1)} %broadcast_in_dim.7), channel_id=1, replica_groups={{0,64,128,192},{1,65,129,193},{2,66,130,194},{3,67,131,195},{4,68,132,1..., dimensions={0} | all-to-all | bytes 147456 | tf_op jit(solution)/shard_map/rest_total/all_to_all | solution.py:245
  95.7 18.1 %all_to_all.23 = f32[32,36,128]{2,1,0:T(8,128)S(1)} all-to-all(f32[32,36,128]{2,1,0:T(8,128)S(1)} %broadcast_in_dim.8), channel_id=1, replica_groups={{0,1,2,3,4,5,6,7,256,257,258,259,260,261,262,263,512,513,514,515,516,51..., dimensions={0} | all-to-all | bytes 1179648 | tf_op jit(solution)/shard_map/plane_gather/all_to_all | solution.py:245
  113.8 7.9 %collective-permute-start.5 = (f32[1152,128]{1,0:T(8,128)S(1)}, f32[1152,128]{1,0:T(8,128)S(1)}, u32[]{:S(2)}, u32[]{:S(2)}) collective-permute-start(f32[1152,128]{1,0:T(8,128)S(1)} %reshape.22), channel_id=1, source_target_pairs={{0,8},{8,0},{1,9},{9,1},{2,10},{10,2},{3,11},{11,3},{4,12},{12,4},... | collective-permute-start | bytes 1769480 | tf_op jit(solution)/shard_map/cores_back/ppermute | solution.py:268
  121.8 1.4 %input_grad.1 = f32[8,32,128]{2,1,0:T(8,128)} custom-call(f32[496,128]{1,0:T(8,128)S(1)} %get-tuple-element.14.first_delta, bf16[2,3,256,384]{3,2,1,0:T(8,128)(2,1)S(1)} %get-tuple-element.13.backward), custom_call_target="tpu_custom_call" | custom-call | flops 2000000000 | bytes 1000000 | tf_op jit(solution)/shard_map/input_grad/pallas_call | solution.py:335
  123.2 0.2 collective-permute-done.5
  123.4 1.1 broadcast_select_fusion
  (19 shorter events, 0.3 us)
Async XLA Ops:
  2.3 19.8 %collective-permute-start = (f32[6,32,128]{2,1,0:T(8,128)S(1)}, f32[6,32,128]{2,1,0:T(8,128)S(1)}, u32[]{:S(2)}, u32[]{:S(2)}) collective-permute-start(f32[6,32,128]{2,1,0:T(8,128)S(1)} %pad_maximum_fusion), channel_id=1, source_target_pairs={{0,8},{8,16},{16,24},{24,32},{32,40},{40,48},{48,56},{56,64},{64,7... | collective-permute-start | bytes 294920 | tf_op jit(solution)/shard_map/ppermute | solution.py:29
  7.7 14.4 %collective-permute-start.1 = (f32[6,32,128]{2,1,0:T(8,128)S(1)}, f32[6,32,128]{2,1,0:T(8,128)S(1)}, u32[]{:S(2)}, u32[]{:S(2)}) collective-permute-start(f32[6,32,128]{2,1,0:T(8,128)S(1)} %pad_maximum_fusion.1), channel_id=1, source_target_pairs={{8,0},{16,8},{24,16},{32,24},{40,32},{48,40},{56,48},{64,56},{72,6... | collective-permute-start | bytes 294920 | tf_op jit(solution)/shard_map/ppermute | solution.py:29
  19.7 1.1 copy-start.2
  20.8 1.1 copy-start.3
  21.8 0.9 copy-start
  21.9 1.0 copy-start.1
  22.8 2.7 %collective-permute-start.2 = (f32[88,128]{1,0:T(8,128)S(1)}, f32[88,128]{1,0:T(8,128)S(1)}, u32[]{:S(2)}, u32[]{:S(2)}) collective-permute-start(f32[88,128]{1,0:T(8,128)S(1)} %get-tuple-element.10), channel_id=1, source_target_pairs={{0,1},{1,2},{2,3},{3,4},{4,5},{5,6},{6,7},{8,9},{9,10},{10,11},{11... | collective-permute-start | bytes 135176 | tf_op jit(solution)/shard_map/ppermute | solution.py:29
  24.1 5.3 %collective-permute-start.3 = (f32[88,128]{1,0:T(8,128)S(1)}, f32[88,128]{1,0:T(8,128)S(1)}, u32[]{:S(2)}, u32[]{:S(2)}) collective-permute-start(f32[88,128]{1,0:T(8,128)S(1)} %get-tuple-element.11), channel_id=1, source_target_pairs={{1,0},{2,1},{3,2},{4,3},{5,4},{6,5},{7,6},{9,8},{10,9},{11,10},{12... | collective-permute-start | bytes 135176 | tf_op jit(solution)/shard_map/ppermute | solution.py:29
  34.7 3.9 %collective-permute-start.4 = (f32[1152,128]{1,0:T(8,128)S(1)}, f32[1152,128]{1,0:T(8,128)S(1)}, u32[]{:S(2)}, u32[]{:S(2)}) collective-permute-start(f32[1152,128]{1,0:T(8,128)S(1)} %get-tuple-element.16), channel_id=1, source_target_pairs={{0,8},{8,0},{1,9},{9,1},{2,10},{10,2},{3,11},{11,3},{4,12},{12,4},... | collective-permute-start | bytes 1769480 | tf_op jit(solution)/shard_map/cores/ppermute | solution.py:257
  113.8 9.6 %collective-permute-start.5 = (f32[1152,128]{1,0:T(8,128)S(1)}, f32[1152,128]{1,0:T(8,128)S(1)}, u32[]{:S(2)}, u32[]{:S(2)}) collective-permute-start(f32[1152,128]{1,0:T(8,128)S(1)} %reshape.22), channel_id=1, source_target_pairs={{0,8},{8,0},{1,9},{9,1},{2,10},{10,2},{3,11},{11,3},{4,12},{12,4},... | collective-permute-start | bytes 1769480 | tf_op jit(solution)/shard_map/cores_back/ppermute | solution.py:268
